TPU v7x, 32 devices: a whole 2x2x4 slice. The times are simulated.
32 devices in a mesh: dp: 4 (over y, core), px: 2 (over x), py: 4 (over z).
Axes of the slice: x: 2, y: 2, z: 4, core: 2. Of those that a mesh axis runs over, the one named last changes fastest.
Arguments:
- state_field: bfloat16 [4, 64, 64, 32, 384], P('dp', 'px', 'py'), may hold values from -6 to 6
- cotangent: bfloat16 [4, 64, 64, 32, 384], P('dp', 'px', 'py'), may hold values from -6 to 6
- first_weight: float32 [2, 4, 96, 96], replicated, may hold values from -0.4375 to 0.4375
- first_bias: float32 [2, 4, 96], replicated, may hold values from -3 to 3
- second_weight: float32 [2, 4, 96, 96], replicated, may hold values from -0.4375 to 0.4375
- second_bias: float32 [2, 4, 96], replicated, may hold values from -3 to 3
Outputs:
- state_grad: bfloat16 [4, 64, 64, 32, 384], P('dp', 'px', 'py')
- first_weight_grad: float32 [2, 4, 96, 96], replicated
- first_bias_grad: float32 [2, 4, 96], replicated
- second_weight_grad: float32 [2, 4, 96, 96], replicated
- second_bias_grad: float32 [2, 4, 96], replicated
All inputs are finite; a program needn't handle non-finite values.
Results may differ from a plain program's by a relative error of at most 0.001.
Values sent between devices are 32-bit elements; how exact they have to be, the bound alone decides.
A program may use at most 320 MiB of HBM per device.

v0:
```python
import math

import jax
import jax.numpy as jnp
from jax import lax
from jax.sharding import PartitionSpec as P

NX = 64
NY = 64
NZ = 32
NB = 4
BS = 96
KZ = 16


shrink_level = 0.25
highest = lax.Precision.HIGHEST


def complex_table(length, modes):
    row_ids = jnp.arange(length, dtype=jnp.int32)[:, None]
    col_ids = jnp.arange(modes, dtype=jnp.int32)[None, :]
    angles = (row_ids * col_ids % length).astype(jnp.float32) * (2.0 * math.pi / length)
    factor = 1.0 / math.sqrt(length)
    cosine = jnp.cos(angles) * factor
    sine_part = jnp.sin(angles) * factor
    upper_half = jnp.stack([cosine, -sine_part], axis=1)
    lower_half = jnp.stack([sine_part, cosine], axis=1)
    return jnp.stack([upper_half, lower_half], axis=0)


def pair_table(weight):
    real_part = weight[0]
    imag_part = weight[1]
    upper_half = jnp.stack([real_part, imag_part], axis=2)
    lower_half = jnp.stack([-imag_part, real_part], axis=2)
    return jnp.stack([upper_half, lower_half], axis=0)


def fold_pairs(pair_grads):
    return jnp.stack(
        [
            pair_grads[0, :, :, 0] + pair_grads[1, :, :, 1],
            pair_grads[0, :, :, 1] - pair_grads[1, :, :, 0],
        ]
    )


def contract(pattern, left_side, right_side):
    return jnp.einsum(
        pattern, left_side, right_side, precision=highest, preferred_element_type=jnp.float32
    )


def along_rows(spectral, rows_table):
    return contract("rmsxyzc,rxqk->qmskyzc", spectral, rows_table)


def along_cols(spectral, cols_table):
    return contract("rmsxyzc,ryqk->qmsxkzc", spectral, cols_table)


def back_rows(spectral, rows_table):
    return contract("qmskyzc,rxqk->rmsxyzc", spectral, rows_table)


def back_cols(spectral, cols_table):
    return contract("qmsxkzc,ryqk->rmsxyzc", spectral, cols_table)


def back_depth(spectral, depth_table):
    return contract("qmsxykc,zqk->msxyzc", spectral, depth_table)


def to_spectrum(fields, depth_table, rows_table, cols_table):
    spectral = contract("msxyzc,zqk->qmsxykc", fields, depth_table)
    spectral = along_cols(
        lax.all_to_all(spectral, "py", split_axis=5, concat_axis=4, tiled=True),
        cols_table=cols_table,
    )
    spectral = along_rows(
        lax.all_to_all(spectral, "px", split_axis=4, concat_axis=3, tiled=True),
        rows_table=rows_table,
    )
    return spectral


def to_field(spectral, depth_table, rows_table, cols_table):
    spectral = back_rows(spectral, rows_table)
    spectral = back_cols(
        lax.all_to_all(spectral, "px", split_axis=3, concat_axis=4, tiled=True),
        cols_table=cols_table,
    )
    result = back_depth(
        lax.all_to_all(spectral, "py", split_axis=4, concat_axis=5, tiled=True),
        depth_table=depth_table,
    )
    return result


def mix_forward(flat_in, first_table, first_bias, second_table, second_bias):
    pre_one = contract("rfbi,rbiqo->qfbo", flat_in, first_table) + first_bias[:, None]
    outer_one, gelu_back = jax.vjp(jax.nn.gelu, pre_one)
    pre_two = contract("rfbi,rbiqo->qfbo", outer_one, second_table) + second_bias[:, None]
    return (outer_one, gelu_back, pre_two)


def shards(state_field, cotangent, first_weight, first_bias, second_weight, second_bias):
    depth_table = complex_table(NZ, KZ)[0]
    rows_table = complex_table(NX, NX)
    cols_table = complex_table(NY, NY)
    full_first = pair_table(first_weight)
    full_second = pair_table(second_weight)
    group_count = NB
    kz_block = lax.axis_index("py")
    kz_local = KZ // lax.axis_size("py")
    kz_global = kz_block * kz_local + jnp.arange(kz_local, dtype=jnp.int32)
    spectral_in = to_spectrum(state_field[None], depth_table, rows_table, cols_table)
    flat_in = spectral_in.reshape(2, -1, group_count, BS)
    outer_one, gelu_back, pre_two = mix_forward(
        flat_in, full_first, first_bias, full_second, second_bias
    )
    raw_gradient = to_spectrum(cotangent[None], depth_table, rows_table, cols_table)
    shape_full = spectral_in.shape
    doubling = jnp.where(kz_global == 0, 1.0, 2.0).astype(jnp.float32)[:, None]
    gradient_in = (raw_gradient * doubling).reshape(2, -1, group_count, BS)
    grad_two = gradient_in * jnp.tanh(pre_two / shrink_level) ** 2
    table_two = contract("rfbi,qfbo->rbiqo", outer_one, grad_two)
    grad_outer = contract("qfbo,rbiqo->rfbi", grad_two, full_second)
    grad_one = gelu_back(grad_outer)[0]
    table_one = contract("rfbi,qfbo->rbiqo", flat_in, grad_one)
    grad_spec = contract("qfbo,rbiqo->rfbi", grad_one, full_first)
    bias_one = jnp.sum(grad_one, axis=1)
    bias_two = jnp.sum(grad_two, axis=1)
    total_freq = state_field.shape[0] * lax.axis_size("dp") * NX * NY * KZ
    norm_factor = 1.0 / math.sqrt(total_freq)
    sums = lax.psum(
        (
            fold_pairs(table_one) * norm_factor,
            bias_one * norm_factor,
            fold_pairs(table_two) * norm_factor,
            bias_two * norm_factor,
        ),
        ("dp", "px", "py"),
    )
    spatial = to_field(grad_spec.reshape(shape_full), depth_table, rows_table, cols_table)[0]
    state_grad = (cotangent.astype(jnp.float32) + spatial).astype(jnp.bfloat16)
    return (state_grad, sums[0], sums[1], sums[2], sums[3])


def solution(mesh):
    in_specs = (
        P("dp", "px", "py", None, None),
        P("dp", "px", "py", None, None),
        P(),
        P(),
        P(),
        P(),
    )
    out_specs = (P("dp", "px", "py", None, None), P(), P(), P(), P())
    return jax.shard_map(shards, mesh=mesh, in_specs=in_specs, out_specs=out_specs, check_vma=False)
```

profile of v0, /device:TPU:0, one launch (start us, length us, event | category | flops | bytes accessed | tf_op | source)
XLA Modules:
  0.0 3237.0 jit_solution(1765777370527135615)
XLA Ops:
  93.0 505.8 %all-to-all-done = f32[2,1,1,32,16,16,384]{6,4,3,0,2,1,5:T(8,128)} async-done(((f32[2,1,1,32,16,16,384]{6,4,3,0,2,1,5:T(8,128)}), f32[2,1,1,32,16,16,384]{6,4,3,0,2,1,5:T(8,128)}, u32[]{:S(2)}, u32[]{:S(2)}) %all-to-all-start) | async-done | bytes 25165856 | tf_op jit(solution)/shard_map/all_to_all | solution.py:78
  626.1 29.8 convolution_bitcast_fusion.3
  682.9 467.1 %all-to-all-done.2 = f32[2,1,1,32,16,16,384]{6,4,3,0,2,1,5:T(8,128)} async-done(((f32[2,1,1,32,16,16,384]{6,4,3,0,2,1,5:T(8,128)}), f32[2,1,1,32,16,16,384]{6,4,3,0,2,1,5:T(8,128)}, u32[]{:S(2)}, u32[]{:S(2)}) %all-to-all-start.2) | async-done | bytes 25165856 | tf_op jit(solution)/shard_map/all_to_all | solution.py:78
  1180.1 29.8 convolution_bitcast_fusion.2
  1237.0 196.5 %all-to-all-done.1 = f32[2,1,1,32,64,4,384]{6,5,3,0,2,1,4:T(4,128)} async-done(((f32[2,1,1,32,64,4,384]{6,5,3,0,2,1,4:T(4,128)}), f32[2,1,1,32,64,4,384]{6,5,3,0,2,1,4:T(4,128)}, u32[]{:S(2)}, u32[]{:S(2)}) %all-to-all-start.1) | async-done | bytes 25165856 | tf_op jit(solution)/shard_map/all_to_all | solution.py:82
  1468.3 29.8 bitcast_multiply_fusion.2
  1498.1 30.3 copy.77
  1528.4 38.3 %reshape.325 = f32[2,8192,4,96]{3,2,1,0:T(4,128)} reshape(f32[2,64,32,4,384]{4,3,2,1,0:T(4,128)} %copy.77) | data formatting | bytes 50331648 | tf_op jit(solution)/shard_map/reshape | solution.py:126
  1566.7 34.9 %copy.86 = f32[2,8192,4,96]{1,3,0,2:T(8,128)} copy(f32[2,8192,4,96]{3,2,1,0:T(4,128)} %reshape.325) | data formatting | bytes 50331648 | tf_op jit(solution)/shard_map/reshape | solution.py:126
  1601.6 114.4 %all-to-all-done.3 = f32[2,1,1,32,64,4,384]{6,5,3,0,2,1,4:T(4,128)} async-done(((f32[2,1,1,32,64,4,384]{6,5,3,0,2,1,4:T(4,128)}), f32[2,1,1,32,64,4,384]{6,5,3,0,2,1,4:T(4,128)}, u32[]{:S(2)}, u32[]{:S(2)}) %all-to-all-start.3) | async-done | bytes 25165856 | tf_op jit(solution)/shard_map/all_to_all | solution.py:82
  1765.1 30.5 copy.82
  1795.5 37.9 %transpose.54 = f32[2,8192,4,96]{3,2,1,0:T(4,128)} reshape(f32[2,64,32,4,384]{4,3,2,1,0:T(4,128)} %copy.82) | data formatting | bytes 50331648 | tf_op jit(solution)/shard_map/reshape;rmsxyzc,rxqk->qmskyzc/transpose | solution.py:119
  1833.5 35.0 %copy.111 = f32[2,8192,4,96,1]{1,3,0,4,2:T(8,128)} copy(f32[2,8192,4,96,1]{3,2,1,0,4:T(4,128)} %bitcast.298) | data formatting | bytes 50331648 | tf_op jit(solution)/shard_map/reshape;rmsxyzc,rxqk->qmskyzc/transpose | solution.py:119
  1896.7 42.2 %fusion.104 = (f32[2,4,96]{2,0,1:T(2,128)}, f32[2,8192,4,96]{1,3,0,2:T(8,128)}) fusion(f32[2,8192,4,96]{1,3,0,2:T(8,128)} %copy.86, f32[2,4,96]{2,0,1:T(2,128)S(1)} %copy-done.19, f32[2,4,96]{2,0,1:T(2,128)S(1)} %copy-done.16, f32[4,2,96,8192,1]{3,2,4,1,0:T(8,128)} %fusion.57, f32[1,4,96,2,96]{2,4,0,3,1:T(8,128)S(1)} %copy-done.9, ...), kind=kOutput, calls=%fused_computation.132 | convolution fusion | flops 14583741440 | bytes 76096512 | tf_op jit(solution)/shard_map/rfbi,rbiqo->qfbo/dot_general | solution.py:50
  1938.9 48.4 %fusion.103 = (f32[2,4,96]{2,0,1:T(2,128)}, f32[2,8192,4,96]{1,3,0,2:T(8,128)}) fusion(f32[2,4,96]{2,0,1:T(2,128)S(1)} %copy-done.16, f32[4,2,96,8192,1]{3,2,4,1,0:T(8,128)} %fusion.57, f32[2,8192,4,96]{1,3,0,2:T(8,128)} %get-tuple-element.39, f32[1,4,96,2,96]{2,4,0,3,1:T(8,128)S(1)} %copy-done.9, f32[1,4,96,2,96]{2,4,0,3,1:T(8,128)S(1)} %copy-done.8), kind=kOutput, calls=%fused_computation.131 | convolution fusion | flops 14627781632 | bytes 76093440 | tf_op jit(solution)/shard_map/qfbo,rbiqo->rfbi/dot_general | solution.py:50
  2015.7 34.2 %copy.89 = f32[2,8192,4,96]{3,2,1,0:T(4,128)} copy(f32[2,8192,4,96]{1,3,0,2:T(8,128)} %fusion.28) | data formatting | bytes 50331648 | tf_op jit(solution)/shard_map/qfbo,rbiqo->rfbi/transpose | solution.py:50
  2049.9 38.5 %reshape.329 = f32[2,64,32,4,384]{4,3,2,1,0:T(4,128)} reshape(f32[2,8192,4,96]{3,2,1,0:T(4,128)} %copy.89) | data formatting | bytes 50331648 | tf_op jit(solution)/shard_map/reshape.22
  2088.4 46.4 %fusion.46 = f32[2,1,1,64,32,4,384]{6,3,5,4,0,2,1:T(8,128)} fusion(f32[2,64,32,4,384]{4,3,2,1,0:T(4,128)} %reshape.329, f32[1,64,2,64]{1,3,0,2:T(8,128)S(1)} %copy-done.5, f32[1,64,2,64]{1,3,0,2:T(8,128)S(1)} %copy-done.3), kind=kOutput, calls=%fused_computation.46 | convolution fusion | flops 9663692800 | bytes 50397184 | tf_op jit(solution)/shard_map/qmskyzc,rxqk->rmsxyzc/dot_general | solution.py:50
  2156.1 276.6 %all_to_all.90 = f32[2,1,1,64,32,4,384]{6,5,4,0,2,1,3:T(4,128)} all-to-all(f32[2,1,1,64,32,4,384]{6,5,4,0,2,1,3:T(4,128)S(1)} %copy.92), channel_id=1, replica_groups=mesh['dp'=4,'px'=2,'py'=4] {'px'}, dimensions={3} | all-to-all | bytes 50331648 | tf_op jit(solution)/shard_map/all_to_all | solution.py:91
  2451.9 29.8 convolution_bitcast_fusion
  2517.3 37.7 %fusion.49 = f32[2,4,96,2,96]{2,4,1,3,0:T(8,128)S(1)} fusion(f32[2,4,96]{2,0,1:T(2,128)S(1)} %copy-done.16, f32[4,2,96,8192,1]{3,2,4,1,0:T(8,128)} %fusion.57, f32[2,8192,4,96]{1,3,0,2:T(8,128)} %get-tuple-element.39), kind=kOutput, calls=%fused_computation.51 | convolution fusion | flops 14552137728 | bytes 50924544 | tf_op jit(solution)/shard_map/rfbi,qfbo->rbiqo/dot_general | solution.py:50
  2555.8 30.9 fusion.54
  2587.6 493.1 %all-reduce = (f32[2,4,96]{2,0,1:T(2,128)S(1)}, f32[2,4,96]{2,0,1:T(2,128)S(1)}) all-reduce(f32[2,4,96]{2,0,1:T(2,128)S(1)} %broadcast_multiply_fusion.1, f32[2,4,96]{2,0,1:T(2,128)S(1)} %broadcast_multiply_fusion), channel_id=1, replica_groups=mesh['dp'=4,'px'=2,'py'=4] {'dp','px','py'}, use_global_device_ids=true, to_apply=%region_2.3 | all-reduce | flops 1536 | bytes 12288 | tf_op jit(solution)/shard_map/psum | solution.py:137
  3081.8 63.4 %all-reduce.4.cloned.1.call-done = (f32[2,4,96,96]{2,3,1,0:T(8,128)}, f32[2,4,96,96]{2,3,1,0:T(8,128)}) async-done(((f32[2,4,96,96]{2,3,1,0:T(8,128)}, f32[2,4,96,96]{2,3,1,0:T(8,128)}), (f32[2,4,96,96]{2,3,1,0:T(8,128)}, f32[2,4,96,96]{2,3,1,0:T(8,128)})) %all-reduce.4.cloned.1.call-update) | async-done | bytes 589840 | tf_op jit(solution)/shard_map/psum | solution.py:137
  (96 shorter events, 501.3 us)
Async XLA Ops:
  7.2 47.2 %copy-start.10 = (f32[32,1,16]{0,2,1:T(8,128)}, f32[32,1,16]{0,2,1:T(8,128)S(1)}, u32[]{:S(2)}) copy-start(f32[32,1,16]{0,2,1:T(8,128)S(1)} %get-tuple-element.40) | copy-start | bytes 6148
  7.2 47.2 %copy-start.12 = (f32[32,1,16]{0,2,1:T(8,128)}, f32[32,1,16]{0,2,1:T(8,128)S(1)}, u32[]{:S(2)}) copy-start(f32[32,1,16]{0,2,1:T(8,128)S(1)} %get-tuple-element.41) | copy-start | bytes 6148
  45.8 552.9 %all-to-all-start = ((f32[2,1,1,32,16,16,384]{6,4,3,0,2,1,5:T(8,128)}), f32[2,1,1,32,16,16,384]{6,4,3,0,2,1,5:T(8,128)}, u32[]{:S(2)}, u32[]{:S(2)}) async-start(f32[2,1,1,32,16,16,384]{6,4,3,0,2,1,5:T(8,128)} %copy.73), calls=%async_computation | async-start | bytes 50331648 | tf_op jit(solution)/shard_map/all_to_all | solution.py:78
  598.7 551.2 %all-to-all-start.2 = ((f32[2,1,1,32,16,16,384]{6,4,3,0,2,1,5:T(8,128)}), f32[2,1,1,32,16,16,384]{6,4,3,0,2,1,5:T(8,128)}, u32[]{:S(2)}, u32[]{:S(2)}) async-start(f32[2,1,1,32,16,16,384]{6,4,3,0,2,1,5:T(8,128)} %copy.78), calls=%async_computation.2 | async-start | bytes 50331648 | tf_op jit(solution)/shard_map/all_to_all | solution.py:78
  607.9 1127.4 %copy-start.2 = (f32[1,64,2,64]{1,3,0,2:T(8,128)}, f32[1,64,2,64]{1,3,0,2:T(8,128)S(1)}, u32[]{:S(2)}) copy-start(f32[1,64,2,64]{1,3,0,2:T(8,128)S(1)} %get-tuple-element.34) | copy-start | bytes 98308
  607.9 1127.4 %copy-start.4 = (f32[1,64,2,64]{1,3,0,2:T(8,128)}, f32[1,64,2,64]{1,3,0,2:T(8,128)S(1)}, u32[]{:S(2)}) copy-start(f32[1,64,2,64]{1,3,0,2:T(8,128)S(1)} %get-tuple-element.35) | copy-start | bytes 98308
  1150.0 283.5 %all-to-all-start.1 = ((f32[2,1,1,32,64,4,384]{6,5,3,0,2,1,4:T(4,128)}), f32[2,1,1,32,64,4,384]{6,5,3,0,2,1,4:T(4,128)}, u32[]{:S(2)}, u32[]{:S(2)}) async-start(f32[2,1,1,32,64,4,384]{6,5,3,0,2,1,4:T(4,128)} %copy.75), calls=%async_computation.1 | async-start | bytes 50331648 | tf_op jit(solution)/shard_map/all_to_all | solution.py:82
  1237.0 208.4 %copy-start.14 = (f32[2,4,96]{2,1,0:T(4,128)S(1)}, f32[2,4,96]{2,1,0:T(4,128)}, u32[]{:S(2)}) copy-start(f32[2,4,96]{2,1,0:T(4,128)} %param.9) | copy-start | bytes 9220
  1237.0 209.0 %copy-start.15 = (f32[2,4,96]{2,1,0:T(4,128)S(1)}, f32[2,4,96]{2,1,0:T(4,128)}, u32[]{:S(2)}) copy-start(f32[2,4,96]{2,1,0:T(4,128)} %param.11) | copy-start | bytes 9220
  1237.0 209.6 %copy-start.6 = (f32[2,4,96,96]{3,2,1,0:T(8,128)S(1)}, f32[2,4,96,96]{3,2,1,0:T(8,128)}, u32[]{:S(2)}) copy-start(f32[2,4,96,96]{3,2,1,0:T(8,128)} %param.8) | copy-start | bytes 884740
  1237.0 209.9 %copy-start.7 = (f32[2,4,96,96]{3,2,1,0:T(8,128)S(1)}, f32[2,4,96,96]{3,2,1,0:T(8,128)}, u32[]{:S(2)}) copy-start(f32[2,4,96,96]{3,2,1,0:T(8,128)} %param.10) | copy-start | bytes 884740
  1433.5 282.6 %all-to-all-start.3 = ((f32[2,1,1,32,64,4,384]{6,5,3,0,2,1,4:T(4,128)}), f32[2,1,1,32,64,4,384]{6,5,3,0,2,1,4:T(4,128)}, u32[]{:S(2)}, u32[]{:S(2)}) async-start(f32[2,1,1,32,64,4,384]{6,5,3,0,2,1,4:T(4,128)} %copy.80), calls=%async_computation.3 | async-start | bytes 50331648 | tf_op jit(solution)/shard_map/all_to_all | solution.py:82
  1833.5 35.0 %copy-start = (f32[1,4,96,2,96]{2,4,0,3,1:T(8,128)S(1)}, f32[1,4,96,2,96]{2,4,0,3,1:T(8,128)}, u32[]{:S(2)}) copy-start(f32[1,4,96,2,96]{2,4,0,3,1:T(8,128)} %get-tuple-element.32) | copy-start | bytes 884740
  1833.5 35.0 %copy-start.1 = (f32[1,4,96,2,96]{2,4,0,3,1:T(8,128)S(1)}, f32[1,4,96,2,96]{2,4,0,3,1:T(8,128)}, u32[]{:S(2)}) copy-start(f32[1,4,96,2,96]{2,4,0,3,1:T(8,128)} %get-tuple-element.33) | copy-start | bytes 884740
  1868.5 28.3 copy-start.8
  1868.5 28.3 copy-start.9
  1868.5 28.3 copy-start.16
  1868.5 28.3 copy-start.19
  2049.9 38.5 %copy-start.3 = (f32[1,64,2,64]{1,3,0,2:T(8,128)S(1)}, f32[1,64,2,64]{1,3,0,2:T(8,128)}, u32[]{:S(2)}) copy-start(f32[1,64,2,64]{1,3,0,2:T(8,128)} %copy-done.2) | copy-start | bytes 98308
  2049.9 38.5 %copy-start.5 = (f32[1,64,2,64]{1,3,0,2:T(8,128)S(1)}, f32[1,64,2,64]{1,3,0,2:T(8,128)}, u32[]{:S(2)}) copy-start(f32[1,64,2,64]{1,3,0,2:T(8,128)} %copy-done.4) | copy-start | bytes 98308
  2508.7 640.4 %all-to-all-start.5 = ((f32[2,1,1,32,64,4,384]{6,5,3,0,2,1,4:T(4,128)}), f32[2,1,1,32,64,4,384]{6,5,3,0,2,1,4:T(4,128)}, u32[]{:S(2)}, u32[]{:S(2)}) async-start(f32[2,1,1,32,64,4,384]{6,5,3,0,2,1,4:T(4,128)} %copy.95), calls=%async_computation.5 | async-start | bytes 50331648 | tf_op jit(solution)/shard_map/all_to_all | solution.py:95
  2517.2 628.0 %all-reduce.4.cloned.1.call-start = ((), (), s32[]{:S(2)}) async-start(), calls=%async_computation.6 | async-start | bytes 1572864 | tf_op jit(solution)/shard_map/psum | solution.py:137
  2555.8 31.7 copy-start.17
  2555.8 31.8 copy-start.18
  (2 other events, 17.1 us)
Sparse Core Ops, SparseCore 0:
  2587.7 557.4 all-reduce.3
where the time goes:
time: 3250 us; the launch traced here: 3240 us
  waiting for transfers between devices  1350 us (42%)
  blocking collectives  770 us (24%)
  local copies, waits for them, and re-layouts  577 us (18%)
  matrix products  475 us (15%)
  starting transfers between devices  49.8 us (2%)
    all_to_all x2, waiting for transfers between devices, to_spectrum(): lax.all_to_all(spectral, 'py', split_axis=5, concat_axis=4, tiled=True)  973 us
    psum x1, blocking collectives, shards(): lax.psum((fold_pairs(table_one) * norm_factor, bias_one * norm_factor, fo...  493 us
    dot_general x15, matrix products, contract(): jnp.einsum(pattern, left_side, right_side, precision=highest, preferred_e...  475 us
    all_to_all x2, waiting for transfers between devices, to_spectrum(): lax.all_to_all(spectral, 'px', split_axis=4, concat_axis=3, tiled=True)  311 us
    all_to_all x1, blocking collectives, to_field(): lax.all_to_all(spectral, 'px', split_axis=3, concat_axis=4, tiled=True)  277 us
    transpose x7, local copies, waits for them, and re-layouts, contract(): jnp.einsum(pattern, left_side, right_side, precision=highest, preferred_e...  179 us
    reshape x2, local copies, waits for them, and re-layouts, shards(): gradient_in = (raw_gradient * doubling).reshape(2, -1, group_count, BS)  73.2 us
    transpose x2, local copies, waits for them, and re-layouts, shards(): flat_in = spectral_in.reshape(2, -1, group_count, BS)  72.9 us
  transfers between devices with their start and end apart: 6, of which 5 were waited for; matrix products, arithmetic and copies ran while one was open for 13% of the time, Pallas kernels for 0%

commit v1 on v0

--- a/solution.py
+++ b/solution.py
@@ -3,6 +3,8 @@
 import jax
 import jax.numpy as jnp
 from jax import lax
+from jax.experimental import pallas as pl
+from jax.experimental.pallas import tpu as pltpu
 from jax.sharding import PartitionSpec as P
 
 NX = 64
@@ -105,7 +107,7 @@
     return (outer_one, gelu_back, pre_two)
 
 
-def shards(state_field, cotangent, first_weight, first_bias, second_weight, second_bias):
+def shards_plain(state_field, cotangent, first_weight, first_bias, second_weight, second_bias):
     depth_table = complex_table(NZ, KZ)[0]
     rows_table = complex_table(NX, NX)
     cols_table = complex_table(NY, NY)
@@ -148,6 +150,544 @@
     return (state_grad, sums[0], sums[1], sums[2], sums[3])
 
 
+C = NB * BS
+LANES = 128
+GROUPS = C // LANES
+CELL_BLOCK = 64
+KY_BLOCK = 8
+VMEM = 60 * 1024 * 1024
+f32 = jnp.float32
+bf16 = jnp.bfloat16
+
+
+def first_group(block):
+    return block * BS // LANES
+
+
+def group_count_of(block):
+    return ((block + 1) * BS - 1) // LANES - first_group(block) + 1
+
+
+WINDOWS = [(first_group(b), group_count_of(b)) for b in range(NB)]
+
+
+def halves(values):
+    high = lax.reduce_precision(values, 8, 7)
+    return high.astype(bf16), (values - high).astype(bf16)
+
+
+def split(values):
+    high = values.astype(bf16)
+    return high, (values - high.astype(f32)).astype(bf16)
+
+
+def dot(left, right, dims=(((1,), (0,)), ((), ()))):
+    return lax.dot_general(left, right, dims, preferred_element_type=f32)
+
+
+def dot3(left, right, dims=(((1,), (0,)), ((), ()))):
+    return (
+        dot(left[0], right[0], dims) + dot(left[1], right[0], dims) + dot(left[0], right[1], dims)
+    )
+
+
+def table_dot(wide, low, values):
+    high, rest = split(values)
+    return dot(wide, jnp.concatenate([high, rest], axis=0)) + dot(low, high)
+
+
+def angle_tables(length, rows, cols):
+    angles = (rows[:, None] * cols[None, :] % length).astype(f32) * (2.0 * math.pi / length)
+    factor = 1.0 / math.sqrt(length)
+    return jnp.cos(angles) * factor, jnp.sin(angles) * factor
+
+
+def table_pair(table):
+    high, low = halves(table)
+    return jnp.concatenate([high, high], axis=1), low
+
+
+def depth_forward(field, table, slots, cells):
+    def body(high_ref, low_ref, field_ref, *outs):
+        for step in range(CELL_BLOCK // 8):
+            part = field_ref[pl.ds(step * 8 * NZ, 8 * NZ), :]
+            result = dot(high_ref[...], part) + dot(low_ref[...], part)
+            for place, out in enumerate(outs):
+                for r in range(2):
+                    row = (place * 2 + r) * 8
+                    out[r, pl.ds(step * 8, 8), :] = result[row : row + 8]
+
+    size = 8 * NZ
+    whole = pl.BlockSpec((size, size), lambda i: (0, 0))
+    return pl.pallas_call(
+        body,
+        grid=(cells // CELL_BLOCK,),
+        in_specs=[whole, whole, pl.BlockSpec((CELL_BLOCK * NZ, C), lambda i: (i, 0))],
+        out_specs=[pl.BlockSpec((2, CELL_BLOCK, C), lambda i: (0, i, 0))] * slots,
+        out_shape=[jax.ShapeDtypeStruct((2, cells, C), f32)] * slots,
+        compiler_params=pltpu.CompilerParams(vmem_limit_bytes=VMEM),
+        cost_estimate=pl.CostEstimate(
+            flops=cells * 32 * C * size * 4, bytes_accessed=cells * 32 * C * 6, transcendentals=0
+        ),
+        name="depth_forward",
+    )(*halves(table), field)
+
+
+def depth_back(parts, cotangent, table, cells):
+    slots = len(parts)
+
+    def body(wide_ref, low_ref, cot_ref, *refs):
+        out = refs[-1]
+        for step in range(CELL_BLOCK // 8):
+            rows = pl.ds(step * 8, 8)
+            stacked = jnp.concatenate(
+                [refs[place][r, rows, :] for place in range(slots) for r in range(2)], axis=0
+            )
+            here = pl.ds(step * 8 * NZ, 8 * NZ)
+            spatial = table_dot(wide_ref[...], low_ref[...], stacked)
+            out[here, :] = (cot_ref[here, :].astype(f32) + spatial).astype(bf16)
+
+    size = 8 * NZ
+    block = pl.BlockSpec((CELL_BLOCK * NZ, C), lambda i: (i, 0))
+    return pl.pallas_call(
+        body,
+        grid=(cells // CELL_BLOCK,),
+        in_specs=[
+            pl.BlockSpec((size, 2 * size), lambda i: (0, 0)),
+            pl.BlockSpec((size, size), lambda i: (0, 0)),
+            block,
+        ]
+        + [pl.BlockSpec((2, CELL_BLOCK, C), lambda i: (0, i, 0))] * slots,
+        out_specs=block,
+        out_shape=jax.ShapeDtypeStruct((cells * NZ, C), bf16),
+        compiler_params=pltpu.CompilerParams(vmem_limit_bytes=VMEM),
+        cost_estimate=pl.CostEstimate(
+            flops=cells * 32 * C * size * 6, bytes_accessed=cells * 32 * C * 8, transcendentals=0
+        ),
+        name="depth_back",
+    )(*table_pair(table), cotangent, *parts)
+
+
+def plane_call(body, operands, in_shapes, out_shapes, rows, name):
+    vmem = pl.BlockSpec(memory_space=pltpu.VMEM)
+    return pl.pallas_call(
+        body,
+        in_specs=[vmem] * len(operands),
+        out_specs=[vmem] * len(out_shapes),
+        out_shape=out_shapes,
+        scratch_shapes=[pltpu.VMEM((GROUPS, rows, LANES), f32)],
+        compiler_params=pltpu.CompilerParams(vmem_limit_bytes=VMEM),
+        cost_estimate=pl.CostEstimate(
+            flops=2 * 2 * NX * NY * C * 256 * 2 * 3,
+            bytes_accessed=2 * NX * NY * C * 8,
+            transcendentals=0,
+        ),
+        name=name,
+    )(*operands)
+
+
+def lanes_of(group):
+    return slice(group * LANES, (group + 1) * LANES)
+
+
+def plane_forward(parts, cols_table, rows_table, nx, ny):
+    xl, yl = NX // nx, NY // ny
+    pitch = NY + 8
+
+    def body(cw, cl, rw, rl, *refs):
+        ins, out, mid = refs[: nx * ny], refs[nx * ny], refs[nx * ny + 1]
+        for dx in range(nx):
+
+            def columns(i, carry, dx=dx):
+                here = pl.ds(pl.multiple_of(i * yl, yl), yl)
+                stacked = jnp.concatenate(
+                    [ins[dx * ny + dy][r, here, :] for r in range(2) for dy in range(ny)], axis=0
+                )
+                result = table_dot(cw[...], cl[...], stacked)
+                for r in range(2):
+                    start = pl.multiple_of(((dx * xl + i) * 2 + r) * pitch, 8)
+                    for g in range(GROUPS):
+                        mid[g, pl.ds(start, NY), :] = result[r * NY : (r + 1) * NY, lanes_of(g)]
+                return carry
+
+            lax.fori_loop(0, xl, columns, 0, unroll=4)
+
+        def across(ky, carry):
+            stacked = jnp.concatenate(
+                [mid[g, pl.ds(ky, 2 * NX, stride=pitch), :] for g in range(GROUPS)], axis=1
+            )
+            out[ky] = table_dot(rw[...], rl[...], stacked).reshape(2, NX, C)
+            return carry
+
+        lax.fori_loop(0, NY, across, 0, unroll=4)
+
+    return plane_call(
+        body,
+        (*table_pair(cols_table), *table_pair(rows_table), *parts),
+        None,
+        [jax.ShapeDtypeStruct((NY, 2, NX, C), f32)],
+        2 * NX * pitch,
+        "plane_forward",
+    )[0]
+
+
+def plane_back(spectrum, cols_table, rows_table, nx, ny):
+    xl, yl = NX // nx, NY // ny
+    pitch = 2 * NX + 8
+
+    def body(cw, cl, rw, rl, spec, *refs):
+        outs, mid = refs[: nx * ny], refs[nx * ny]
+
+        def across(ky, carry):
+            result = table_dot(rw[...], rl[...], spec[ky].reshape(2 * NX, C))
+            start = pl.multiple_of(ky * pitch, 8)
+            for g in range(GROUPS):
+                mid[g, pl.ds(start, 2 * NX), :] = result[:, lanes_of(g)]
+            return carry
+
+        lax.fori_loop(0, NY, across, 0, unroll=4)
+        for dx in range(nx):
+
+            def columns(i, carry, dx=dx):
+                stacked = jnp.concatenate(
+                    [
+                        jnp.concatenate(
+                            [
+                                mid[g, pl.ds((dx * xl + i) * 2 + r, NY, stride=pitch), :]
+                                for g in range(GROUPS)
+                            ],
+                            axis=1,
+                        )
+                        for r in range(2)
+                    ],
+                    axis=0,
+                )
+                result = table_dot(cw[...], cl[...], stacked)
+                here = pl.ds(pl.multiple_of(i * yl, yl), yl)
+                for r in range(2):
+                    for dy in range(ny):
+                        row = (r * ny + dy) * yl
+                        outs[dx * ny + dy][r, here, :] = result[row : row + yl]
+                return carry
+
+            lax.fori_loop(0, xl, columns, 0, unroll=4)
+
+    return plane_call(
+        body,
+        (*table_pair(cols_table), *table_pair(rows_table), spectrum),
+        None,
+        [jax.ShapeDtypeStruct((2, xl * yl, C), f32)] * (nx * ny),
+        NY * pitch,
+        "plane_back",
+    )
+
+
+def window(pair, block):
+    start, count = WINDOWS[block]
+    lanes = slice(start * LANES, (start + count) * LANES)
+    return jnp.concatenate([pair[0][:, lanes], pair[1][:, lanes]], axis=1)
+
+
+def spread(results):
+    sides = []
+    for r in range(2):
+        groups = [None] * GROUPS
+        for block, result in enumerate(results):
+            start, count = WINDOWS[block]
+            for g in range(count):
+                at = r * count + g
+                part = result[:, at * LANES : (at + 1) * LANES]
+                groups[start + g] = part if groups[start + g] is None else groups[start + g] + part
+        sides.append(jnp.concatenate(groups, axis=1))
+    return sides
+
+
+def offset_of(block):
+    return block * BS - WINDOWS[block][0] * LANES
+
+
+def stack_windows(table, axes):
+    pieces = []
+    for block in range(NB):
+        count = WINDOWS[block][1]
+        before = offset_of(block)
+        wide = (before, count * LANES - before - BS)
+        slim = (0, LANES - BS)
+        sides = (wide, slim) if axes == 0 else (slim, wide)
+        piece = jnp.pad(table[:, block], ((0, 0), sides[0], (0, 0), sides[1]))
+        piece = piece.reshape(2 * piece.shape[1], -1)
+        pieces.append(piece)
+    return jnp.concatenate(pieces, axis=axes)
+
+
+def unstack_windows(stacked, axes):
+    pieces = []
+    at = 0
+    for block in range(NB):
+        count = WINDOWS[block][1]
+        size = 2 * count * LANES
+        before = offset_of(block)
+        if axes == 0:
+            piece = stacked[at : at + size].reshape(2, count * LANES, 2, LANES)
+            piece = piece[:, before : before + BS, :, :BS]
+        else:
+            piece = stacked[:, at : at + size].reshape(2, LANES, 2, count * LANES)
+            piece = piece[:, :BS, :, before : before + BS]
+        pieces.append(piece)
+        at += size
+    return jnp.stack(pieces, axis=1)
+
+
+OFFSETS = [sum(2 * w[1] * LANES for w in WINDOWS[:b]) for b in range(NB + 1)]
+WIDE = OFFSETS[NB]
+SLIM = 2 * LANES
+
+
+def block_span(block):
+    return slice(OFFSETS[block], OFFSETS[block + 1])
+
+
+def slim_span(block):
+    return slice(block * SLIM, (block + 1) * SLIM)
+
+
+def plane_block():
+    return pl.BlockSpec((KY_BLOCK, 2, NX, C), lambda i: (i, 0, 0, 0))
+
+
+def whole_block(*shape):
+    return pl.BlockSpec(shape, lambda i: (0,) * len(shape))
+
+
+def mix_cost(count, reads):
+    rows = NX * NY
+    return pl.CostEstimate(
+        flops=rows * WIDE * SLIM * 2 * 3 * count,
+        bytes_accessed=rows * 2 * C * 4 * reads,
+        transcendentals=rows * 2 * C * 2,
+    )
+
+
+def both_sides(ref):
+    rows = KY_BLOCK * NX
+    return ref[:, 0].reshape(rows, C), ref[:, 1].reshape(rows, C)
+
+
+def mix_front(spectrum, first, first_bias, second, second_bias):
+    rows = KY_BLOCK * NX
+    slope = math.sqrt(2.0 / math.pi)
+
+    def body(fh, fl, fb, sh, sl, sb, spec, high_ref, low_ref, deriv_ref, gate_ref):
+        sides = [split(side) for side in both_sides(spec)]
+        results = []
+        for b in range(NB):
+            left = tuple(window((sides[0][k], sides[1][k]), b) for k in range(2))
+            v = dot3(left, (fh[block_span(b), :], fl[block_span(b), :]))
+            v = v + fb[:, slim_span(b)]
+            square = v * v
+            t = jnp.tanh(slope * (v + 0.044715 * (v * square)))
+            upper = 0.5 * (1.0 + t)
+            outer = split(v * upper)
+            high_ref[:, slim_span(b)] = outer[0]
+            low_ref[:, slim_span(b)] = outer[1]
+            deriv_ref[:, slim_span(b)] = upper + (0.5 * slope) * v * (1.0 - t * t) * (
+                1.0 + (3 * 0.044715) * square
+            )
+            results.append(dot3(outer, (sh[:, block_span(b)], sl[:, block_span(b)])))
+        for r, side in enumerate(spread(results)):
+            t = jnp.tanh((side + sb[r : r + 1, :]) * (1.0 / shrink_level))
+            gate_ref[:, r] = (t * t).reshape(KY_BLOCK, NX, C)
+
+    slim = pl.BlockSpec((rows, NB * SLIM), lambda i: (i, 0))
+    total = NX * NY
+    return pl.pallas_call(
+        body,
+        grid=(NY // KY_BLOCK,),
+        in_specs=[
+            whole_block(WIDE, SLIM),
+            whole_block(WIDE, SLIM),
+            whole_block(1, NB * SLIM),
+            whole_block(SLIM, WIDE),
+            whole_block(SLIM, WIDE),
+            whole_block(2, C),
+            plane_block(),
+        ],
+        out_specs=[slim, slim, slim, plane_block()],
+        out_shape=[
+            jax.ShapeDtypeStruct((total, NB * SLIM), bf16),
+            jax.ShapeDtypeStruct((total, NB * SLIM), bf16),
+            jax.ShapeDtypeStruct((total, NB * SLIM), f32),
+            jax.ShapeDtypeStruct((NY, 2, NX, C), f32),
+        ],
+        compiler_params=pltpu.CompilerParams(vmem_limit_bytes=VMEM),
+        cost_estimate=mix_cost(2, 5),
+        name="mix_front",
+    )(*first, first_bias, *second, second_bias, spectrum)
+
+
+def mix_back(gradient, spectrum, kept, first_back, second_back):
+    rows = KY_BLOCK * NX
+    along = (((0,), (0,)), ((), ()))
+
+    def body(
+        fh, fl, sh, sl, grad, spec, high_ref, low_ref, deriv_ref, gate_ref,
+        out, one_ref, two_ref, bias_one_ref, bias_two_ref,
+    ):
+        @pl.when(pl.program_id(0) == 0)
+        def _():
+            for ref in (one_ref, two_ref, bias_one_ref, bias_two_ref):
+                ref[...] = jnp.zeros_like(ref)
+
+        grads = [g * t for g, t in zip(both_sides(grad), both_sides(gate_ref))]
+        for r in range(2):
+            bias_two_ref[r] += jnp.sum(grads[r].reshape(rows // 8, 8, C), axis=0)
+        grads = [split(g) for g in grads]
+        sides = [split(side) for side in both_sides(spec)]
+        results = []
+        for b in range(NB):
+            two = tuple(window((grads[0][k], grads[1][k]), b) for k in range(2))
+            outer = (high_ref[:, slim_span(b)], low_ref[:, slim_span(b)])
+            two_ref[:, block_span(b)] += dot3(outer, two, along)
+            one = dot3(two, (sh[block_span(b), :], sl[block_span(b), :]))
+            one = one * deriv_ref[:, slim_span(b)]
+            bias_one_ref[:, slim_span(b)] += jnp.sum(one.reshape(rows // 8, 8, SLIM), axis=0)
+            one = split(one)
+            left = tuple(window((sides[0][k], sides[1][k]), b) for k in range(2))
+            one_ref[block_span(b), :] += dot3(left, one, along)
+            results.append(dot3(one, (fh[:, block_span(b)], fl[:, block_span(b)])))
+        for r, side in enumerate(spread(results)):
+            out[:, r] = side.reshape(KY_BLOCK, NX, C)
+
+    slim = pl.BlockSpec((rows, NB * SLIM), lambda i: (i, 0))
+    return pl.pallas_call(
+        body,
+        grid=(NY // KY_BLOCK,),
+        in_specs=[
+            whole_block(SLIM, WIDE),
+            whole_block(SLIM, WIDE),
+            whole_block(WIDE, SLIM),
+            whole_block(WIDE, SLIM),
+            plane_block(),
+            plane_block(),
+            slim,
+            slim,
+            slim,
+            plane_block(),
+        ],
+        out_specs=[
+            plane_block(),
+            whole_block(WIDE, SLIM),
+            whole_block(SLIM, WIDE),
+            whole_block(8, NB * SLIM),
+            whole_block(2, 8, C),
+        ],
+        out_shape=[
+            jax.ShapeDtypeStruct((NY, 2, NX, C), f32),
+            jax.ShapeDtypeStruct((WIDE, SLIM), f32),
+            jax.ShapeDtypeStruct((SLIM, WIDE), f32),
+            jax.ShapeDtypeStruct((8, NB * SLIM), f32),
+            jax.ShapeDtypeStruct((2, 8, C), f32),
+        ],
+        compiler_params=pltpu.CompilerParams(vmem_limit_bytes=VMEM),
+        cost_estimate=mix_cost(4, 7),
+        name="mix_back",
+    )(*first_back, *second_back, gradient, spectrum, *kept)
+
+
+def shards_planes(state_field, cotangent, first_weight, first_bias, second_weight, second_bias):
+    nx, ny = lax.axis_size("px"), lax.axis_size("py")
+    me_x, me_y = lax.axis_index("px"), lax.axis_index("py")
+    places = [(dx, dy) for dx in range(nx) for dy in range(ny)]
+    chunks = KZ // (nx * ny)
+    xl, yl = NX // nx, NY // ny
+    cells = xl * yl
+
+    owner = jnp.stack([(me_x + dx) % nx * ny + (me_y + dy) % ny for dx, dy in places])
+    kz = (owner[:, None] * chunks + jnp.arange(chunks, dtype=jnp.int32)).reshape(-1)
+    cosine, sine = angle_tables(NZ, kz, jnp.arange(NZ, dtype=jnp.int32))
+    depth = jnp.stack([cosine, -sine], axis=1)
+    eye = jnp.eye(8, dtype=f32)
+    depth = jnp.einsum("krz,ij->krijz", depth, eye, precision=highest)
+    doubling = jnp.where(kz == 0, 1.0, 2.0).astype(f32)[:, None, None, None, None]
+    size = 8 * NZ
+    depth_table = depth.reshape(size, size)
+    depth_doubled = (depth * doubling).reshape(size, size)
+
+    x_at = ((me_x - jnp.arange(nx)) % nx)[:, None] * xl + jnp.arange(xl)
+    y_at = ((me_y - jnp.arange(ny)) % ny)[:, None] * yl + jnp.arange(yl)
+    cosine, sine = angle_tables(NY, jnp.arange(NY), y_at.reshape(-1))
+    cols_table = jnp.concatenate(
+        [jnp.concatenate([cosine, sine], axis=1), jnp.concatenate([-sine, cosine], axis=1)], axis=0
+    )
+    cosine, sine = angle_tables(NX, jnp.arange(NX), x_at.reshape(-1))
+    rows_table = jnp.concatenate(
+        [
+            jnp.stack([cosine, sine], axis=2).reshape(NX, 2 * NX),
+            jnp.stack([-sine, cosine], axis=2).reshape(NX, 2 * NX),
+        ],
+        axis=0,
+    )
+
+    def moved(value, place, way):
+        dx, dy = place
+        if dx == 0 and dy == 0:
+            return value
+        pairs = [
+            (a * ny + b, (a + way * dx) % nx * ny + (b + way * dy) % ny)
+            for a in range(nx)
+            for b in range(ny)
+        ]
+        return lax.ppermute(value, ("px", "py"), pairs)
+
+    def spectra(field, table):
+        parts = depth_forward(field.reshape(cells * NZ, C), table, len(places) * chunks, cells)
+        arrived = [
+            [moved(parts[at * chunks + j], place, 1) for at, place in enumerate(places)]
+            for j in range(chunks)
+        ]
+        return [plane_forward(arrived[j], cols_table, rows_table, nx, ny) for j in range(chunks)]
+
+    full_first = pair_table(first_weight)
+    full_second = pair_table(second_weight)
+    first = stack_windows(full_first, 0)
+    second = stack_windows(full_second, 1)
+    slim_bias = jnp.pad(first_bias, ((0, 0), (0, 0), (0, LANES - BS)))
+    slim_bias = jnp.transpose(slim_bias, (1, 0, 2)).reshape(1, NB * SLIM)
+    wide_bias = second_bias.reshape(2, C)
+
+    spectrum = spectra(state_field, depth_table)
+    kept = [mix_front(s, halves(first), slim_bias, halves(second), wide_bias) for s in spectrum]
+    gradient = spectra(cotangent, depth_doubled)
+    backs = [
+        mix_back(g, s, k, halves(first.T), halves(second.T))
+        for g, s, k in zip(gradient, spectrum, kept)
+    ]
+    total_freq = state_field.shape[0] * lax.axis_size("dp") * NX * NY * KZ
+    norm_factor = 1.0 / math.sqrt(total_freq)
+    table_one, table_two, bias_one, bias_two = [
+        sum(back[i] for back in backs) * norm_factor for i in range(1, 5)
+    ]
+    bias_one = jnp.sum(bias_one, axis=0).reshape(NB, 2, LANES)[:, :, :BS]
+    sums = lax.psum(
+        (
+            fold_pairs(unstack_windows(table_one, 0)),
+            jnp.transpose(bias_one, (1, 0, 2)),
+            fold_pairs(unstack_windows(table_two, 1)),
+            jnp.sum(bias_two, axis=1).reshape(2, NB, BS),
+        ),
+        ("dp", "px", "py"),
+    )
+    returned = [None] * (len(places) * chunks)
+    for j in range(chunks):
+        parts = plane_back(backs[j][0], cols_table.T, rows_table.T, nx, ny)
+        for at, place in enumerate(places):
+            returned[at * chunks + j] = moved(parts[at], place, -1)
+    state_grad = depth_back(
+        returned, cotangent.reshape(cells * NZ, C), depth_table.T, cells
+    ).reshape(cotangent.shape)
+    return (state_grad, sums[0], sums[1], sums[2], sums[3])
+
+
 def solution(mesh):
     in_specs = (
         P("dp", "px", "py", None, None),
@@ -158,4 +698,6 @@
         P(),
     )
     out_specs = (P("dp", "px", "py", None, None), P(), P(), P(), P())
+    planes = KZ % (mesh.shape["px"] * mesh.shape["py"]) == 0
+    shards = shards_planes if planes else shards_plain
     return jax.shard_map(shards, mesh=mesh, in_specs=in_specs, out_specs=out_specs, check_vma=False)

time: 3250 us -> 1850 us (0.57)
  waiting for transfers between devices: 1350 us -> 564 us
  starting transfers between devices: 49.8 us -> 699 us
  blocking collectives: 770 us -> 121 us
  local copies, waits for them, and re-layouts: 577 us -> 39.6 us
  matrix products: 475 us -> 0 us
  Pallas kernels: 0 us -> 387 us
    all_to_all x5 -> x0, waiting for transfers between devices: 1280 us -> none  [the longest x2 973 us: to_spectrum(): lax.all_to_all(spectral, 'py', split_axis=5, concat_axis=4, tiled=True)]
    ppermute x0 -> x42, starting transfers between devices: none -> 699 us  [moved(): return lax.ppermute(value, ('px', 'py'), pairs)]
    dot_general x15 -> x0, matrix products: 475 us -> none  [contract(): jnp.einsum(pattern, left_side, right_side, precision=highest, preferred_e...]
    ppermute x0 -> x42, waiting for transfers between devices: none -> 457 us  [moved(): return lax.ppermute(value, ('px', 'py'), pairs)]
    pallas_call x0 -> x13, Pallas kernels: none -> 387 us  [the longest x6 140 us: plane_call(): pl.pallas_call(body, in_specs=[vmem] * len(operands), out_specs=[vmem] *...]
    psum x1, blocking collectives: 493 us -> 121 us  [shards_planes(): lax.psum((fold_pairs(unstack_windows(table_one, 0)), jnp.transpose(bias_o...]
    all_to_all x1 -> x0, blocking collectives: 277 us -> none  [to_field(): lax.all_to_all(spectral, 'px', split_axis=3, concat_axis=4, tiled=True)]
    transpose x9 -> x3, local copies, waits for them, and re-layouts: 252 us -> 0.61 us  [the longest x2 0.6 us: shards_planes(): slim_bias = jnp.transpose(slim_bias, (1, 0, 2)).reshape(1, NB * SLIM)]
  transfers between devices with their start and end apart: 6 -> 43, of which waited for: 5 -> 8; matrix products, arithmetic and copies ran while one was open for 13% -> 3% of each run, Pallas kernels for 0% -> 20%
where the time goes in v1:
time: 1850 us; the launch traced here: 1840 us
  starting transfers between devices  699 us (38%)
  waiting for transfers between devices  564 us (30%)
  Pallas kernels  387 us (21%)
  blocking collectives  121 us (7%)
  local copies, waits for them, and re-layouts  39.6 us (2%)
    ppermute x42, starting transfers between devices, moved(): return lax.ppermute(value, ('px', 'py'), pairs)  699 us
    ppermute x42, waiting for transfers between devices, moved(): return lax.ppermute(value, ('px', 'py'), pairs)  457 us
    pallas_call x6, Pallas kernels, plane_call(): pl.pallas_call(body, in_specs=[vmem] * len(operands), out_specs=[vmem] *...  140 us
    psum x1, blocking collectives, shards_planes(): lax.psum((fold_pairs(unstack_windows(table_one, 0)), jnp.transpose(bias_o...  121 us
    pallas_call x2, Pallas kernels, mix_back(): pl.pallas_call(body, grid=(NY // KY_BLOCK,), in_specs=[whole_block(SLIM,...  112 us
    psum x1, waiting for transfers between devices, shards_planes(): lax.psum((fold_pairs(unstack_windows(table_one, 0)), jnp.transpose(bias_o...  107 us
    pallas_call x2, Pallas kernels, mix_front(): pl.pallas_call(body, grid=(NY // KY_BLOCK,), in_specs=[whole_block(WIDE,...  77.4 us
  transfers between devices with their start and end apart: 43, of which 8 were waited for; matrix products, arithmetic and copies ran while one was open for 3% of the time, Pallas kernels for 20%

profile of v1, /device:TPU:0, one launch (start us, length us, event | category | flops | bytes accessed | tf_op | source)
XLA Modules:
  0.0 1842.1 jit_solution(13061085726135840657)
XLA Ops:
  75.9 61.0 %collective-permute-start.26 = (f32[2,512,384]{2,1,0:T(8,128)}, f32[2,512,384]{2,1,0:T(8,128)}, u32[]{:S(2)}, u32[]{:S(2)}) collective-permute-start(f32[2,512,384]{2,1,0:T(8,128)} %get-tuple-element.107), channel_id=1, source_target_pairs={{0,6},{1,7},{2,4},{3,5},{4,2},{5,3},{6,0},{7,1},{8,14},{9,15},{10,... | collective-permute-start | bytes 4718600 | tf_op jit(solution)/shard_map/ppermute | solution.py:640
  137.0 85.2 %collective-permute-start.27 = (f32[2,512,384]{2,1,0:T(8,128)}, f32[2,512,384]{2,1,0:T(8,128)}, u32[]{:S(2)}, u32[]{:S(2)}) collective-permute-start(f32[2,512,384]{2,1,0:T(8,128)} %get-tuple-element.108), channel_id=1, source_target_pairs={{0,7},{1,4},{2,5},{3,6},{4,3},{5,0},{6,1},{7,2},{8,15},{9,12},{10,... | collective-permute-start | bytes 4718600 | tf_op jit(solution)/shard_map/ppermute | solution.py:640
  222.1 30.7 %collective-permute-start.14 = (f32[2,512,384]{2,1,0:T(8,128)}, f32[2,512,384]{2,1,0:T(8,128)}, u32[]{:S(2)}, u32[]{:S(2)}) collective-permute-start(f32[2,512,384]{2,1,0:T(8,128)} %get-tuple-element.94), channel_id=1, source_target_pairs={{0,1},{1,2},{2,3},{3,0},{4,5},{5,6},{6,7},{7,4},{8,9},{9,10},{10,1... | collective-permute-start | bytes 4718600 | tf_op jit(solution)/shard_map/ppermute | solution.py:640
  266.0 71.5 %collective-permute-done.26.refs_6_ = f32[2,512,384]{2,1,0:T(8,128)} collective-permute-done((f32[2,512,384]{2,1,0:T(8,128)}, f32[2,512,384]{2,1,0:T(8,128)}, u32[]{:S(2)}, u32[]{:S(2)}) %collective-permute-start.26) | collective-permute-done | bytes 1572896 | tf_op jit(solution)/shard_map/ppermute | solution.py:640
  338.0 41.1 %collective-permute-start.18 = (f32[2,512,384]{2,1,0:T(8,128)}, f32[2,512,384]{2,1,0:T(8,128)}, u32[]{:S(2)}, u32[]{:S(2)}) collective-permute-start(f32[2,512,384]{2,1,0:T(8,128)} %get-tuple-element.98), channel_id=1, source_target_pairs={{0,5},{1,6},{2,7},{3,4},{4,1},{5,2},{6,3},{7,0},{8,13},{9,14},{10,... | collective-permute-start | bytes 4718600 | tf_op jit(solution)/shard_map/ppermute | solution.py:640
  379.1 35.2 %collective-permute-start.19 = (f32[2,512,384]{2,1,0:T(8,128)}, f32[2,512,384]{2,1,0:T(8,128)}, u32[]{:S(2)}, u32[]{:S(2)}) collective-permute-start(f32[2,512,384]{2,1,0:T(8,128)} %get-tuple-element.99), channel_id=1, source_target_pairs={{0,6},{1,7},{2,4},{3,5},{4,2},{5,3},{6,0},{7,1},{8,14},{9,15},{10,... | collective-permute-start | bytes 4718600 | tf_op jit(solution)/shard_map/ppermute | solution.py:640
  414.2 57.1 %collective-permute-done.15.refs_2_ = f32[2,512,384]{2,1,0:T(8,128)} collective-permute-done((f32[2,512,384]{2,1,0:T(8,128)}, f32[2,512,384]{2,1,0:T(8,128)}, u32[]{:S(2)}, u32[]{:S(2)}) %collective-permute-start.15) | collective-permute-done | bytes 1572896 | tf_op jit(solution)/shard_map/ppermute | solution.py:640
  512.2 95.0 %collective-permute-done.19.refs_6_ = f32[2,512,384]{2,1,0:T(8,128)} collective-permute-done((f32[2,512,384]{2,1,0:T(8,128)}, f32[2,512,384]{2,1,0:T(8,128)}, u32[]{:S(2)}, u32[]{:S(2)}) %collective-permute-start.19) | collective-permute-done | bytes 1572896 | tf_op jit(solution)/shard_map/ppermute | solution.py:640
  607.7 42.1 %collective-permute-start.11 = (f32[2,512,384]{2,1,0:T(8,128)}, f32[2,512,384]{2,1,0:T(8,128)}, u32[]{:S(2)}, u32[]{:S(2)}) collective-permute-start(f32[2,512,384]{2,1,0:T(8,128)} %get-tuple-element.84), channel_id=1, source_target_pairs={{0,5},{1,6},{2,7},{3,4},{4,1},{5,2},{6,3},{7,0},{8,13},{9,14},{10,... | collective-permute-start | bytes 4718600 | tf_op jit(solution)/shard_map/ppermute | solution.py:640
  673.5 38.8 %mix_front.3 = (bf16[4096,1024]{1,0:T(8,128)(2,1)}, bf16[4096,1024]{1,0:T(8,128)(2,1)}, f32[4096,1024]{1,0:T(8,128)}, f32[64,2,64,384]{3,2,1,0:T(8,128)}) custom-call(bf16[1536,256]{1,0:T(8,128)(2,1)} %copy.119.fh, bf16[1536,256]{1,0:T(8,128)(2,1)} %copy.120.fl, f32[1,1024]{1,0:T(1,128)} %bitcast.164, bf16[256,1536]{1,0:T(8,128)(2,1)} %copy.121.sh, ...), custom_call_target="tpu_custom_call" | custom-call | flops 19327352832 | bytes 62914560 | tf_op jit(solution)/shard_map/mix_front/pallas_call | solution.py:503
  716.7 53.9 %collective-permute-start.13 = (f32[2,512,384]{2,1,0:T(8,128)S(1)}, f32[2,512,384]{2,1,0:T(8,128)}, u32[]{:S(2)}, u32[]{:S(2)}) collective-permute-start(f32[2,512,384]{2,1,0:T(8,128)S(1)} %copy-done.22), channel_id=1, source_target_pairs={{0,7},{1,4},{2,5},{3,6},{4,3},{5,0},{6,1},{7,2},{8,15},{9,12},{10,... | collective-permute-start | bytes 4718600 | tf_op jit(solution)/shard_map/ppermute | solution.py:640
  770.5 55.7 %mix_back.3 = (f32[64,2,64,384]{3,2,1,0:T(8,128)}, f32[1536,256]{1,0:T(8,128)}, f32[256,1536]{1,0:T(8,128)}, f32[8,1024]{1,0:T(8,128)}, f32[2,8,384]{2,1,0:T(8,128)}) custom-call(bf16[256,1536]{1,0:T(8,128)(2,1)} %get-tuple-element.168.fh, bf16[256,1536]{1,0:T(8,128)(2,1)} %get-tuple-element.167.fl, bf16[1536,256]{1,0:T(8,128)(2,1)} %get-tuple-element.166.sh, ...), custom_call_target="tpu_custom_call" | custom-call | flops 38654705664 | bytes 88080384 | tf_op jit(solution)/shard_map/mix_back/pallas_call | solution.py:562
  874.4 46.8 %collective-permute-start.4 = (f32[2,512,384]{2,1,0:T(8,128)}, f32[2,512,384]{2,1,0:T(8,128)}, u32[]{:S(2)}, u32[]{:S(2)}) collective-permute-start(f32[2,512,384]{2,1,0:T(8,128)} %get-tuple-element.76), channel_id=1, source_target_pairs={{0,5},{1,6},{2,7},{3,4},{4,1},{5,2},{6,3},{7,0},{8,13},{9,14},{10,... | collective-permute-start | bytes 4718600 | tf_op jit(solution)/shard_map/ppermute | solution.py:640
  955.9 54.8 %collective-permute-done.1.refs_2_ = f32[2,512,384]{2,1,0:T(8,128)} collective-permute-done((f32[2,512,384]{2,1,0:T(8,128)}, f32[2,512,384]{2,1,0:T(8,128)}, u32[]{:S(2)}, u32[]{:S(2)}) %collective-permute-start.1) | collective-permute-done | bytes 1572896 | tf_op jit(solution)/shard_map/ppermute | solution.py:640
  1024.3 38.6 %mix_front.2 = (bf16[4096,1024]{1,0:T(8,128)(2,1)}, bf16[4096,1024]{1,0:T(8,128)(2,1)}, f32[4096,1024]{1,0:T(8,128)}, f32[64,2,64,384]{3,2,1,0:T(8,128)}) custom-call(bf16[1536,256]{1,0:T(8,128)(2,1)} %copy.119.fh, bf16[1536,256]{1,0:T(8,128)(2,1)} %copy.120.fl, f32[1,1024]{1,0:T(1,128)} %bitcast.165, bf16[256,1536]{1,0:T(8,128)(2,1)} %copy.121.sh, ...), custom_call_target="tpu_custom_call" | custom-call | flops 19327352832 | bytes 62914560 | tf_op jit(solution)/shard_map/mix_front/pallas_call | solution.py:503
  1063.0 93.5 %collective-permute-start.33 = (f32[2,512,384]{2,1,0:T(8,128)}, f32[2,512,384]{2,1,0:T(8,128)}, u32[]{:S(2)}, u32[]{:S(2)}) collective-permute-start(f32[2,512,384]{2,1,0:T(8,128)} %get-tuple-element.120), channel_id=1, source_target_pairs={{0,1},{1,2},{2,3},{3,0},{4,5},{5,6},{6,7},{7,4},{8,9},{9,10},{10,1... | collective-permute-start | bytes 4718600 | tf_op jit(solution)/shard_map/ppermute | solution.py:640
  1157.6 37.7 %collective-permute-start.37 = (f32[2,512,384]{2,1,0:T(8,128)}, f32[2,512,384]{2,1,0:T(8,128)}, u32[]{:S(2)}, u32[]{:S(2)}) collective-permute-start(f32[2,512,384]{2,1,0:T(8,128)} %get-tuple-element.124), channel_id=1, source_target_pairs={{0,7},{1,4},{2,5},{3,6},{4,3},{5,0},{6,1},{7,2},{8,15},{9,12},{10,... | collective-permute-start | bytes 4718600 | tf_op jit(solution)/shard_map/ppermute | solution.py:640
  1219.0 55.9 %mix_back.2 = (f32[64,2,64,384]{3,2,1,0:T(8,128)}, f32[1536,256]{1,0:T(8,128)}, f32[256,1536]{1,0:T(8,128)}, f32[8,1024]{1,0:T(8,128)}, f32[2,8,384]{2,1,0:T(8,128)}) custom-call(bf16[256,1536]{1,0:T(8,128)(2,1)} %get-tuple-element.168.fh, bf16[256,1536]{1,0:T(8,128)(2,1)} %get-tuple-element.167.fl, bf16[1536,256]{1,0:T(8,128)(2,1)} %get-tuple-element.166.sh, ...), custom_call_target="tpu_custom_call" | custom-call | flops 38654705664 | bytes 88080384 | tf_op jit(solution)/shard_map/mix_back/pallas_call | solution.py:562
  1312.6 93.6 %collective-permute-done.39.refs_13_ = f32[2,512,384]{2,1,0:T(8,128)S(1)} collective-permute-done((f32[2,512,384]{2,1,0:T(8,128)}, f32[2,512,384]{2,1,0:T(8,128)S(1)}, u32[]{:S(2)}, u32[]{:S(2)}) %collective-permute-start.39) | collective-permute-done | bytes 1572896 | tf_op jit(solution)/shard_map/ppermute | solution.py:640
  1407.3 31.5 %collective-permute-start.36 = (f32[2,512,384]{2,1,0:T(8,128)}, f32[2,512,384]{2,1,0:T(8,128)}, u32[]{:S(2)}, u32[]{:S(2)}) collective-permute-start(f32[2,512,384]{2,1,0:T(8,128)} %get-tuple-element.123), channel_id=1, source_target_pairs={{0,7},{1,4},{2,5},{3,6},{4,3},{5,0},{6,1},{7,2},{8,15},{9,12},{10,... | collective-permute-start | bytes 4718600 | tf_op jit(solution)/shard_map/ppermute | solution.py:640
  1438.8 69.0 %collective-permute-start.38 = (f32[2,512,384]{2,1,0:T(8,128)}, f32[2,512,384]{2,1,0:T(8,128)}, u32[]{:S(2)}, u32[]{:S(2)}) collective-permute-start(f32[2,512,384]{2,1,0:T(8,128)} %get-tuple-element.125), channel_id=1, source_target_pairs={{0,6},{1,7},{2,4},{3,5},{4,2},{5,3},{6,0},{7,1},{8,14},{9,15},{10,... | collective-permute-start | bytes 4718600 | tf_op jit(solution)/shard_map/ppermute | solution.py:640
  1507.8 63.4 %collective-permute-done.30.refs_4_ = f32[2,512,384]{2,1,0:T(8,128)} collective-permute-done((f32[2,512,384]{2,1,0:T(8,128)}, f32[2,512,384]{2,1,0:T(8,128)}, u32[]{:S(2)}, u32[]{:S(2)}) %collective-permute-start.30) | collective-permute-done | bytes 1572896 | tf_op jit(solution)/shard_map/ppermute | solution.py:640
  1573.0 120.6 %all-reduce.9 = (f32[2,4,96]{2,0,1:T(2,128)S(1)}, f32[2,4,96]{2,1,0:T(4,128)}) all-reduce(f32[2,4,96]{2,0,1:T(2,128)S(1)} %slice_bitcast_fusion.4, f32[2,4,96]{2,1,0:T(4,128)S(1)} %reshape.597), channel_id=1, replica_groups=mesh['dp'=4,'px'=2,'py'=4] {'dp','px','py'}, use_global_device_ids=true, to_apply=%region_2.3 | all-reduce | flops 1536 | bytes 12288 | tf_op jit(solution)/shard_map/psum | solution.py:671
  1724.3 107.2 %all-reduce.13.cloned.1.call-done = (f32[2,4,96,96]{3,2,1,0:T(8,128)}, f32[2,4,96,96]{3,2,1,0:T(8,128)}) async-done(((f32[2,4,96,96]{3,2,1,0:T(8,128)}, f32[2,4,96,96]{3,2,1,0:T(8,128)}), (f32[2,4,96,96]{3,2,1,0:T(8,128)}, f32[2,4,96,96]{3,2,1,0:T(8,128)})) %all-reduce.13.cloned.1.call-update) | async-done | bytes 589840 | tf_op jit(solution)/shard_map/psum | solution.py:671
  (256 shorter events, 347.2 us)
Async XLA Ops:
  7.2 1824.3 %all-reduce.13.cloned.1.call-start = ((), (), s32[]{:S(2)}) async-start(), calls=%async_computation | async-start | bytes 1572864 | tf_op jit(solution)/shard_map/psum | solution.py:671
  32.6 189.6 %collective-permute-start.23 = (f32[2,512,384]{2,1,0:T(8,128)}, f32[2,512,384]{2,1,0:T(8,128)}, u32[]{:S(2)}, u32[]{:S(2)}) collective-permute-start(f32[2,512,384]{2,1,0:T(8,128)} %get-tuple-element.104), channel_id=1, source_target_pairs={{0,3},{1,0},{2,1},{3,2},{4,7},{5,4},{6,5},{7,6},{8,11},{9,8},{10,9... | collective-permute-start | bytes 4718600 | tf_op jit(solution)/shard_map/ppermute | solution.py:640
  33.9 218.9 %collective-permute-start.24 = (f32[2,512,384]{2,1,0:T(8,128)}, f32[2,512,384]{2,1,0:T(8,128)}, u32[]{:S(2)}, u32[]{:S(2)}) collective-permute-start(f32[2,512,384]{2,1,0:T(8,128)} %get-tuple-element.105), channel_id=1, source_target_pairs={{0,4},{1,5},{2,6},{3,7},{4,0},{5,1},{6,2},{7,3},{8,12},{9,13},{10,... | collective-permute-start | bytes 4718600 | tf_op jit(solution)/shard_map/ppermute | solution.py:640
  35.4 228.2 %collective-permute-start.25 = (f32[2,512,384]{2,1,0:T(8,128)}, f32[2,512,384]{2,1,0:T(8,128)}, u32[]{:S(2)}, u32[]{:S(2)}) collective-permute-start(f32[2,512,384]{2,1,0:T(8,128)} %get-tuple-element.106), channel_id=1, source_target_pairs={{0,5},{1,6},{2,7},{3,4},{4,1},{5,2},{6,3},{7,0},{8,13},{9,14},{10,... | collective-permute-start | bytes 4718600 | tf_op jit(solution)/shard_map/ppermute | solution.py:640
  75.9 261.5 %collective-permute-start.26 = (f32[2,512,384]{2,1,0:T(8,128)}, f32[2,512,384]{2,1,0:T(8,128)}, u32[]{:S(2)}, u32[]{:S(2)}) collective-permute-start(f32[2,512,384]{2,1,0:T(8,128)} %get-tuple-element.107), channel_id=1, source_target_pairs={{0,6},{1,7},{2,4},{3,5},{4,2},{5,3},{6,0},{7,1},{8,14},{9,15},{10,... | collective-permute-start | bytes 4718600 | tf_op jit(solution)/shard_map/ppermute | solution.py:640
  137.0 201.0 %collective-permute-start.27 = (f32[2,512,384]{2,1,0:T(8,128)}, f32[2,512,384]{2,1,0:T(8,128)}, u32[]{:S(2)}, u32[]{:S(2)}) collective-permute-start(f32[2,512,384]{2,1,0:T(8,128)} %get-tuple-element.108), channel_id=1, source_target_pairs={{0,7},{1,4},{2,5},{3,6},{4,3},{5,0},{6,1},{7,2},{8,15},{9,12},{10,... | collective-permute-start | bytes 4718600 | tf_op jit(solution)/shard_map/ppermute | solution.py:640
  252.8 218.6 %collective-permute-start.15 = (f32[2,512,384]{2,1,0:T(8,128)}, f32[2,512,384]{2,1,0:T(8,128)}, u32[]{:S(2)}, u32[]{:S(2)}) collective-permute-start(f32[2,512,384]{2,1,0:T(8,128)} %get-tuple-element.95), channel_id=1, source_target_pairs={{0,2},{1,3},{2,0},{3,1},{4,6},{5,7},{6,4},{7,5},{8,10},{9,11},{10,... | collective-permute-start | bytes 4718600 | tf_op jit(solution)/shard_map/ppermute | solution.py:640
  263.6 244.7 %collective-permute-start.16 = (f32[2,512,384]{2,1,0:T(8,128)}, f32[2,512,384]{2,1,0:T(8,128)S(1)}, u32[]{:S(2)}, u32[]{:S(2)}) collective-permute-start(f32[2,512,384]{2,1,0:T(8,128)} %get-tuple-element.96), channel_id=1, source_target_pairs={{0,3},{1,0},{2,1},{3,2},{4,7},{5,4},{6,5},{7,6},{8,11},{9,8},{10,9... | collective-permute-start | bytes 4718600 | tf_op jit(solution)/shard_map/ppermute | solution.py:640
  379.1 228.1 %collective-permute-start.19 = (f32[2,512,384]{2,1,0:T(8,128)}, f32[2,512,384]{2,1,0:T(8,128)}, u32[]{:S(2)}, u32[]{:S(2)}) collective-permute-start(f32[2,512,384]{2,1,0:T(8,128)} %get-tuple-element.99), channel_id=1, source_target_pairs={{0,6},{1,7},{2,4},{3,5},{4,2},{5,3},{6,0},{7,1},{8,14},{9,15},{10,... | collective-permute-start | bytes 4718600 | tf_op jit(solution)/shard_map/ppermute | solution.py:640
  508.3 204.0 %collective-permute-start.7 = (f32[2,512,384]{2,1,0:T(8,128)}, f32[2,512,384]{2,1,0:T(8,128)}, u32[]{:S(2)}, u32[]{:S(2)}) collective-permute-start(f32[2,512,384]{2,1,0:T(8,128)} %get-tuple-element.80), channel_id=1, source_target_pairs={{0,1},{1,2},{2,3},{3,0},{4,5},{5,6},{6,7},{7,4},{8,9},{9,10},{10,1... | collective-permute-start | bytes 4718600 | tf_op jit(solution)/shard_map/ppermute | solution.py:640
  508.4 208.3 %collective-permute-start.8 = (f32[2,512,384]{2,1,0:T(8,128)}, f32[2,512,384]{2,1,0:T(8,128)}, u32[]{:S(2)}, u32[]{:S(2)}) collective-permute-start(f32[2,512,384]{2,1,0:T(8,128)} %get-tuple-element.81), channel_id=1, source_target_pairs={{0,2},{1,3},{2,0},{3,1},{4,6},{5,7},{6,4},{7,5},{8,10},{9,11},{10,... | collective-permute-start | bytes 4718600 | tf_op jit(solution)/shard_map/ppermute | solution.py:640
  508.5 317.8 %collective-permute-start.9 = (f32[2,512,384]{2,1,0:T(8,128)}, f32[2,512,384]{2,1,0:T(8,128)}, u32[]{:S(2)}, u32[]{:S(2)}) collective-permute-start(f32[2,512,384]{2,1,0:T(8,128)} %get-tuple-element.82), channel_id=1, source_target_pairs={{0,3},{1,0},{2,1},{3,2},{4,7},{5,4},{6,5},{7,6},{8,11},{9,8},{10,9... | collective-permute-start | bytes 4718600 | tf_op jit(solution)/shard_map/ppermute | solution.py:640
  607.2 219.5 %collective-permute-start.10 = (f32[2,512,384]{2,1,0:T(8,128)}, f32[2,512,384]{2,1,0:T(8,128)}, u32[]{:S(2)}, u32[]{:S(2)}) collective-permute-start(f32[2,512,384]{2,1,0:T(8,128)} %get-tuple-element.83), channel_id=1, source_target_pairs={{0,4},{1,5},{2,6},{3,7},{4,0},{5,1},{6,2},{7,3},{8,12},{9,13},{10,... | collective-permute-start | bytes 4718600 | tf_op jit(solution)/shard_map/ppermute | solution.py:640
  607.7 241.8 %collective-permute-start.11 = (f32[2,512,384]{2,1,0:T(8,128)}, f32[2,512,384]{2,1,0:T(8,128)}, u32[]{:S(2)}, u32[]{:S(2)}) collective-permute-start(f32[2,512,384]{2,1,0:T(8,128)} %get-tuple-element.84), channel_id=1, source_target_pairs={{0,5},{1,6},{2,7},{3,4},{4,1},{5,2},{6,3},{7,0},{8,13},{9,14},{10,... | collective-permute-start | bytes 4718600 | tf_op jit(solution)/shard_map/ppermute | solution.py:640
  849.5 213.3 %collective-permute-start.2 = (f32[2,512,384]{2,1,0:T(8,128)}, f32[2,512,384]{2,1,0:T(8,128)}, u32[]{:S(2)}, u32[]{:S(2)}) collective-permute-start(f32[2,512,384]{2,1,0:T(8,128)} %get-tuple-element.74), channel_id=1, source_target_pairs={{0,3},{1,0},{2,1},{3,2},{4,7},{5,4},{6,5},{7,6},{8,11},{9,8},{10,9... | collective-permute-start | bytes 4718600 | tf_op jit(solution)/shard_map/ppermute | solution.py:640
  944.9 211.7 %collective-permute-start.5 = (f32[2,512,384]{2,1,0:T(8,128)S(1)}, f32[2,512,384]{2,1,0:T(8,128)}, u32[]{:S(2)}, u32[]{:S(2)}) collective-permute-start(f32[2,512,384]{2,1,0:T(8,128)S(1)} %copy-done.25), channel_id=1, source_target_pairs={{0,6},{1,7},{2,4},{3,5},{4,2},{5,3},{6,0},{7,1},{8,14},{9,15},{10,... | collective-permute-start | bytes 4718600 | tf_op jit(solution)/shard_map/ppermute | solution.py:640
  1062.9 240.2 %collective-permute-start.29 = (f32[2,512,384]{2,1,0:T(8,128)}, f32[2,512,384]{2,1,0:T(8,128)}, u32[]{:S(2)}, u32[]{:S(2)}) collective-permute-start(f32[2,512,384]{2,1,0:T(8,128)} %get-tuple-element.116), channel_id=1, source_target_pairs={{0,3},{1,0},{2,1},{3,2},{4,7},{5,4},{6,5},{7,6},{8,11},{9,8},{10,9... | collective-permute-start | bytes 4718600 | tf_op jit(solution)/shard_map/ppermute | solution.py:640
  1063.0 240.2 %collective-permute-start.31 = (f32[2,512,384]{2,1,0:T(8,128)}, f32[2,512,384]{2,1,0:T(8,128)}, u32[]{:S(2)}, u32[]{:S(2)}) collective-permute-start(f32[2,512,384]{2,1,0:T(8,128)} %get-tuple-element.118), channel_id=1, source_target_pairs={{0,2},{1,3},{2,0},{3,1},{4,6},{5,7},{6,4},{7,5},{8,10},{9,11},{10,... | collective-permute-start | bytes 4718600 | tf_op jit(solution)/shard_map/ppermute | solution.py:640
  1063.0 241.1 %collective-permute-start.33 = (f32[2,512,384]{2,1,0:T(8,128)}, f32[2,512,384]{2,1,0:T(8,128)}, u32[]{:S(2)}, u32[]{:S(2)}) collective-permute-start(f32[2,512,384]{2,1,0:T(8,128)} %get-tuple-element.120), channel_id=1, source_target_pairs={{0,1},{1,2},{2,3},{3,0},{4,5},{5,6},{6,7},{7,4},{8,9},{9,10},{10,1... | collective-permute-start | bytes 4718600 | tf_op jit(solution)/shard_map/ppermute | solution.py:640
  1307.5 263.7 %collective-permute-start.30 = (f32[2,512,384]{2,1,0:T(8,128)}, f32[2,512,384]{2,1,0:T(8,128)}, u32[]{:S(2)}, u32[]{:S(2)}) collective-permute-start(f32[2,512,384]{2,1,0:T(8,128)} %get-tuple-element.117), channel_id=1, source_target_pairs={{0,2},{1,3},{2,0},{3,1},{4,6},{5,7},{6,4},{7,5},{8,10},{9,11},{10,... | collective-permute-start | bytes 4718600 | tf_op jit(solution)/shard_map/ppermute | solution.py:640
  1312.6 389.4 %collective-permute-start.32 = (f32[2,512,384]{2,1,0:T(8,128)}, f32[2,512,384]{2,1,0:T(8,128)}, u32[]{:S(2)}, u32[]{:S(2)}) collective-permute-start(f32[2,512,384]{2,1,0:T(8,128)} %get-tuple-element.119), channel_id=1, source_target_pairs={{0,1},{1,2},{2,3},{3,0},{4,5},{5,6},{6,7},{7,4},{8,9},{9,10},{10,1... | collective-permute-start | bytes 4718600 | tf_op jit(solution)/shard_map/ppermute | solution.py:640
  1406.2 295.8 %collective-permute-start.34 = (f32[2,512,384]{2,1,0:T(8,128)}, f32[2,512,384]{2,1,0:T(8,128)}, u32[]{:S(2)}, u32[]{:S(2)}) collective-permute-start(f32[2,512,384]{2,1,0:T(8,128)} %get-tuple-element.121), channel_id=1, source_target_pairs={{0,4},{1,5},{2,6},{3,7},{4,0},{5,1},{6,2},{7,3},{8,12},{9,13},{10,... | collective-permute-start | bytes 4718600 | tf_op jit(solution)/shard_map/ppermute | solution.py:640
  1407.3 294.7 %collective-permute-start.36 = (f32[2,512,384]{2,1,0:T(8,128)}, f32[2,512,384]{2,1,0:T(8,128)}, u32[]{:S(2)}, u32[]{:S(2)}) collective-permute-start(f32[2,512,384]{2,1,0:T(8,128)} %get-tuple-element.123), channel_id=1, source_target_pairs={{0,7},{1,4},{2,5},{3,6},{4,3},{5,0},{6,1},{7,2},{8,15},{9,12},{10,... | collective-permute-start | bytes 4718600 | tf_op jit(solution)/shard_map/ppermute | solution.py:640
  1438.8 263.2 %collective-permute-start.38 = (f32[2,512,384]{2,1,0:T(8,128)}, f32[2,512,384]{2,1,0:T(8,128)}, u32[]{:S(2)}, u32[]{:S(2)}) collective-permute-start(f32[2,512,384]{2,1,0:T(8,128)} %get-tuple-element.125), channel_id=1, source_target_pairs={{0,6},{1,7},{2,4},{3,5},{4,2},{5,3},{6,0},{7,1},{8,14},{9,15},{10,... | collective-permute-start | bytes 4718600 | tf_op jit(solution)/shard_map/ppermute | solution.py:640
  (46 other events, 4051.6 us)
Sparse Core Ops, SparseCore 0:
  1702.1 129.3 all-reduce.12

commit v2 on v1

--- a/solution.py
+++ b/solution.py
@@ -668,20 +668,29 @@
         sum(back[i] for back in backs) * norm_factor for i in range(1, 5)
     ]
     bias_one = jnp.sum(bias_one, axis=0).reshape(NB, 2, LANES)[:, :, :BS]
-    sums = lax.psum(
-        (
-            fold_pairs(unstack_windows(table_one, 0)),
-            jnp.transpose(bias_one, (1, 0, 2)),
-            fold_pairs(unstack_windows(table_two, 1)),
-            jnp.sum(bias_two, axis=1).reshape(2, NB, BS),
-        ),
-        ("dp", "px", "py"),
-    )
+    shares = (
+        fold_pairs(unstack_windows(table_one, 0)),
+        jnp.transpose(bias_one, (1, 0, 2)),
+        fold_pairs(unstack_windows(table_two, 1)),
+        jnp.sum(bias_two, axis=1).reshape(2, NB, BS),
+    )
+    packed = jnp.concatenate([share.reshape(-1) for share in shares]).reshape(-1, LANES)
+    packed, last_back = lax.optimization_barrier((packed, backs[-1][0]))
+    packed = lax.psum(packed, ("dp", "px", "py"))
     returned = [None] * (len(places) * chunks)
     for j in range(chunks):
-        parts = plane_back(backs[j][0], cols_table.T, rows_table.T, nx, ny)
+        spectral = last_back if j == chunks - 1 else backs[j][0]
+        parts = plane_back(spectral, cols_table.T, rows_table.T, nx, ny)
         for at, place in enumerate(places):
-            returned[at * chunks + j] = moved(parts[at], place, -1)
+            part = parts[at]
+            if j == chunks - 1 and at == len(places) - 1:
+                part, packed = lax.optimization_barrier((part, packed))
+            returned[at * chunks + j] = moved(part, place, -1)
+    packed = packed.reshape(-1)
+    sums = []
+    for share in shares:
+        sums.append(packed[: share.size].reshape(share.shape))
+        packed = packed[share.size :]
     state_grad = depth_back(
         returned, cotangent.reshape(cells * NZ, C), depth_table.T, cells
     ).reshape(cotangent.shape)

time: 1850 us -> 1890 us (1.022)
  waiting for transfers between devices: 564 us -> 810 us
  blocking collectives: 121 us -> 0 us
  starting transfers between devices: 699 us -> 613 us
    ppermute x42, waiting for transfers between devices: 457 us -> 609 us  [moved(): return lax.ppermute(value, ('px', 'py'), pairs)]
    psum x1 -> x0, blocking collectives: 121 us -> none  [shards_planes(): lax.psum((fold_pairs(unstack_windows(table_one, 0)), jnp.transpose(bias_o...]
    psum x1, waiting for transfers between devices: 107 us -> 201 us  [shards_planes(): packed = lax.psum(packed, ('dp', 'px', 'py'))]
    ppermute x42, starting transfers between devices: 699 us -> 613 us  [moved(): return lax.ppermute(value, ('px', 'py'), pairs)]
  transfers between devices with their start and end apart: 43 -> 43, of which waited for: 8 -> 12; matrix products, arithmetic and copies ran while one was open for 3% -> 2% of each run, Pallas kernels for 20% -> 13%
where the time goes in v2:
time: 1890 us; the launch traced here: 1880 us
  waiting for transfers between devices  810 us (43%)
  starting transfers between devices  613 us (32%)
  Pallas kernels  387 us (20%)
  local copies, waits for them, and re-layouts  40.7 us (2%)
    ppermute x42, starting transfers between devices, moved(): return lax.ppermute(value, ('px', 'py'), pairs)  613 us
    ppermute x42, waiting for transfers between devices, moved(): return lax.ppermute(value, ('px', 'py'), pairs)  609 us
    psum x1, waiting for transfers between devices, shards_planes(): packed = lax.psum(packed, ('dp', 'px', 'py'))  201 us
    pallas_call x6, Pallas kernels, plane_call(): pl.pallas_call(body, in_specs=[vmem] * len(operands), out_specs=[vmem] *...  140 us
    pallas_call x2, Pallas kernels, mix_back(): pl.pallas_call(body, grid=(NY // KY_BLOCK,), in_specs=[whole_block(SLIM,...  112 us
    pallas_call x2, Pallas kernels, mix_front(): pl.pallas_call(body, grid=(NY // KY_BLOCK,), in_specs=[whole_block(WIDE,...  77.6 us
  transfers between devices with their start and end apart: 43, of which 12 were waited for; matrix products, arithmetic and copies ran while one was open for 2% of the time, Pallas kernels for 13%

profile of v2, /device:TPU:0, one launch (start us, length us, event | category | flops | bytes accessed | tf_op | source)
XLA Modules:
  0.0 1881.9 jit_solution(5552904627236099581)
XLA Ops:
  75.7 61.2 %collective-permute-start.26 = (f32[2,512,384]{2,1,0:T(8,128)}, f32[2,512,384]{2,1,0:T(8,128)}, u32[]{:S(2)}, u32[]{:S(2)}) collective-permute-start(f32[2,512,384]{2,1,0:T(8,128)} %get-tuple-element.112), channel_id=1, source_target_pairs={{0,6},{1,7},{2,4},{3,5},{4,2},{5,3},{6,0},{7,1},{8,14},{9,15},{10,... | collective-permute-start | bytes 4718600 | tf_op jit(solution)/shard_map/ppermute | solution.py:640
  137.0 85.2 %collective-permute-start.27 = (f32[2,512,384]{2,1,0:T(8,128)}, f32[2,512,384]{2,1,0:T(8,128)}, u32[]{:S(2)}, u32[]{:S(2)}) collective-permute-start(f32[2,512,384]{2,1,0:T(8,128)} %get-tuple-element.113), channel_id=1, source_target_pairs={{0,7},{1,4},{2,5},{3,6},{4,3},{5,0},{6,1},{7,2},{8,15},{9,12},{10,... | collective-permute-start | bytes 4718600 | tf_op jit(solution)/shard_map/ppermute | solution.py:640
  222.1 30.7 %collective-permute-start.14 = (f32[2,512,384]{2,1,0:T(8,128)}, f32[2,512,384]{2,1,0:T(8,128)}, u32[]{:S(2)}, u32[]{:S(2)}) collective-permute-start(f32[2,512,384]{2,1,0:T(8,128)} %get-tuple-element.99), channel_id=1, source_target_pairs={{0,1},{1,2},{2,3},{3,0},{4,5},{5,6},{6,7},{7,4},{8,9},{9,10},{10,1... | collective-permute-start | bytes 4718600 | tf_op jit(solution)/shard_map/ppermute | solution.py:640
  263.9 73.5 %collective-permute-done.26.refs_6_ = f32[2,512,384]{2,1,0:T(8,128)} collective-permute-done((f32[2,512,384]{2,1,0:T(8,128)}, f32[2,512,384]{2,1,0:T(8,128)}, u32[]{:S(2)}, u32[]{:S(2)}) %collective-permute-start.26) | collective-permute-done | bytes 1572896 | tf_op jit(solution)/shard_map/ppermute | solution.py:640
  338.0 41.1 %collective-permute-start.18 = (f32[2,512,384]{2,1,0:T(8,128)}, f32[2,512,384]{2,1,0:T(8,128)}, u32[]{:S(2)}, u32[]{:S(2)}) collective-permute-start(f32[2,512,384]{2,1,0:T(8,128)} %get-tuple-element.103), channel_id=1, source_target_pairs={{0,5},{1,6},{2,7},{3,4},{4,1},{5,2},{6,3},{7,0},{8,13},{9,14},{10,... | collective-permute-start | bytes 4718600 | tf_op jit(solution)/shard_map/ppermute | solution.py:640
  379.0 35.2 %collective-permute-start.19 = (f32[2,512,384]{2,1,0:T(8,128)}, f32[2,512,384]{2,1,0:T(8,128)}, u32[]{:S(2)}, u32[]{:S(2)}) collective-permute-start(f32[2,512,384]{2,1,0:T(8,128)} %get-tuple-element.104), channel_id=1, source_target_pairs={{0,6},{1,7},{2,4},{3,5},{4,2},{5,3},{6,0},{7,1},{8,14},{9,15},{10,... | collective-permute-start | bytes 4718600 | tf_op jit(solution)/shard_map/ppermute | solution.py:640
  414.2 57.1 %collective-permute-done.15.refs_2_ = f32[2,512,384]{2,1,0:T(8,128)} collective-permute-done((f32[2,512,384]{2,1,0:T(8,128)}, f32[2,512,384]{2,1,0:T(8,128)}, u32[]{:S(2)}, u32[]{:S(2)}) %collective-permute-start.15) | collective-permute-done | bytes 1572896 | tf_op jit(solution)/shard_map/ppermute | solution.py:640
  512.1 95.1 %collective-permute-done.19.refs_6_ = f32[2,512,384]{2,1,0:T(8,128)} collective-permute-done((f32[2,512,384]{2,1,0:T(8,128)}, f32[2,512,384]{2,1,0:T(8,128)}, u32[]{:S(2)}, u32[]{:S(2)}) %collective-permute-start.19) | collective-permute-done | bytes 1572896 | tf_op jit(solution)/shard_map/ppermute | solution.py:640
  607.7 42.1 %collective-permute-start.11 = (f32[2,512,384]{2,1,0:T(8,128)}, f32[2,512,384]{2,1,0:T(8,128)}, u32[]{:S(2)}, u32[]{:S(2)}) collective-permute-start(f32[2,512,384]{2,1,0:T(8,128)} %get-tuple-element.88), channel_id=1, source_target_pairs={{0,5},{1,6},{2,7},{3,4},{4,1},{5,2},{6,3},{7,0},{8,13},{9,14},{10,... | collective-permute-start | bytes 4718600 | tf_op jit(solution)/shard_map/ppermute | solution.py:640
  673.5 39.0 %mix_front.3 = (bf16[4096,1024]{1,0:T(8,128)(2,1)}, bf16[4096,1024]{1,0:T(8,128)(2,1)}, f32[4096,1024]{1,0:T(8,128)}, f32[64,2,64,384]{3,2,1,0:T(8,128)}) custom-call(bf16[1536,256]{1,0:T(8,128)(2,1)} %copy.149.fh, bf16[1536,256]{1,0:T(8,128)(2,1)} %copy.150.fl, f32[1,1024]{1,0:T(1,128)} %bitcast.178, bf16[256,1536]{1,0:T(8,128)(2,1)} %copy.151.sh, ...), custom_call_target="tpu_custom_call" | custom-call | flops 19327352832 | bytes 62914560 | tf_op jit(solution)/shard_map/mix_front/pallas_call | solution.py:503
  719.1 56.3 %collective-permute-start = (f32[2,512,384]{2,1,0:T(8,128)}, f32[2,512,384]{2,1,0:T(8,128)}, u32[]{:S(2)}, u32[]{:S(2)}) collective-permute-start(f32[2,512,384]{2,1,0:T(8,128)} %get-tuple-element.76), channel_id=1, source_target_pairs={{0,1},{1,2},{2,3},{3,0},{4,5},{5,6},{6,7},{7,4},{8,9},{9,10},{10,1... | collective-permute-start | bytes 4718600 | tf_op jit(solution)/shard_map/ppermute | solution.py:640
  775.4 55.7 %mix_back.3 = (f32[64,2,64,384]{3,2,1,0:T(8,128)}, f32[1536,256]{1,0:T(8,128)}, f32[256,1536]{1,0:T(8,128)}, f32[8,1024]{1,0:T(8,128)}, f32[2,8,384]{2,1,0:T(8,128)}) custom-call(bf16[256,1536]{1,0:T(8,128)(2,1)} %get-tuple-element.162.fh, bf16[256,1536]{1,0:T(8,128)(2,1)} %get-tuple-element.161.fl, bf16[1536,256]{1,0:T(8,128)(2,1)} %get-tuple-element.160.sh, ...), custom_call_target="tpu_custom_call" | custom-call | flops 38654705664 | bytes 88080384 | tf_op jit(solution)/shard_map/mix_back/pallas_call | solution.py:562
  833.7 43.2 %collective-permute-done.12.refs_6_ = f32[2,512,384]{2,1,0:T(8,128)} collective-permute-done((f32[2,512,384]{2,1,0:T(8,128)S(1)}, f32[2,512,384]{2,1,0:T(8,128)}, u32[]{:S(2)}, u32[]{:S(2)}) %collective-permute-start.12) | collective-permute-done | bytes 1572896 | tf_op jit(solution)/shard_map/ppermute | solution.py:640
  877.4 42.9 %collective-permute-start.4 = (f32[2,512,384]{2,1,0:T(8,128)}, f32[2,512,384]{2,1,0:T(8,128)}, u32[]{:S(2)}, u32[]{:S(2)}) collective-permute-start(f32[2,512,384]{2,1,0:T(8,128)} %get-tuple-element.80), channel_id=1, source_target_pairs={{0,5},{1,6},{2,7},{3,4},{4,1},{5,2},{6,3},{7,0},{8,13},{9,14},{10,... | collective-permute-start | bytes 4718600 | tf_op jit(solution)/shard_map/ppermute | solution.py:640
  955.0 55.8 %collective-permute-done.1.refs_2_ = f32[2,512,384]{2,1,0:T(8,128)} collective-permute-done((f32[2,512,384]{2,1,0:T(8,128)}, f32[2,512,384]{2,1,0:T(8,128)}, u32[]{:S(2)}, u32[]{:S(2)}) %collective-permute-start.1) | collective-permute-done | bytes 1572896 | tf_op jit(solution)/shard_map/ppermute | solution.py:640
  1023.4 38.6 %mix_front.2 = (bf16[4096,1024]{1,0:T(8,128)(2,1)}, bf16[4096,1024]{1,0:T(8,128)(2,1)}, f32[4096,1024]{1,0:T(8,128)}, f32[64,2,64,384]{3,2,1,0:T(8,128)}) custom-call(bf16[1536,256]{1,0:T(8,128)(2,1)} %copy.149.fh, bf16[1536,256]{1,0:T(8,128)(2,1)} %copy.150.fl, f32[1,1024]{1,0:T(1,128)} %bitcast.179, bf16[256,1536]{1,0:T(8,128)(2,1)} %copy.151.sh, ...), custom_call_target="tpu_custom_call" | custom-call | flops 19327352832 | bytes 62914560 | tf_op jit(solution)/shard_map/mix_front/pallas_call | solution.py:503
  1110.4 56.0 %mix_back.2 = (f32[64,2,64,384]{3,2,1,0:T(8,128)}, f32[1536,256]{1,0:T(8,128)}, f32[256,1536]{1,0:T(8,128)}, f32[8,1024]{1,0:T(8,128)}, f32[2,8,384]{2,1,0:T(8,128)}) custom-call(bf16[256,1536]{1,0:T(8,128)(2,1)} %get-tuple-element.162.fh, bf16[256,1536]{1,0:T(8,128)(2,1)} %get-tuple-element.161.fl, bf16[1536,256]{1,0:T(8,128)(2,1)} %get-tuple-element.160.sh, ...), custom_call_target="tpu_custom_call" | custom-call | flops 38654705664 | bytes 88080384 | tf_op jit(solution)/shard_map/mix_back/pallas_call | solution.py:562
  1201.6 37.3 %collective-permute-start.29 = (f32[2,512,384]{2,1,0:T(8,128)}, f32[2,512,384]{2,1,0:T(8,128)S(1)}, u32[]{:S(2)}, u32[]{:S(2)}) collective-permute-start(f32[2,512,384]{2,1,0:T(8,128)} %get-tuple-element.129), channel_id=1, source_target_pairs={{0,3},{1,0},{2,1},{3,2},{4,7},{5,4},{6,5},{7,6},{8,11},{9,8},{10,9... | collective-permute-start | bytes 4718600 | tf_op jit(solution)/shard_map/ppermute | solution.py:640
  1275.5 99.8 %collective-permute-done.31.refs_5_ = f32[2,512,384]{2,1,0:T(8,128)S(1)} collective-permute-done((f32[2,512,384]{2,1,0:T(8,128)}, f32[2,512,384]{2,1,0:T(8,128)S(1)}, u32[]{:S(2)}, u32[]{:S(2)}) %collective-permute-start.31) | collective-permute-done | bytes 1572896 | tf_op jit(solution)/shard_map/ppermute | solution.py:640
  1375.3 52.8 %collective-permute-start.28 = (f32[2,512,384]{2,1,0:T(8,128)}, f32[2,512,384]{2,1,0:T(8,128)}, u32[]{:S(2)}, u32[]{:S(2)}) collective-permute-start(f32[2,512,384]{2,1,0:T(8,128)} %get-tuple-element.128), channel_id=1, source_target_pairs={{0,3},{1,0},{2,1},{3,2},{4,7},{5,4},{6,5},{7,6},{8,11},{9,8},{10,9... | collective-permute-start | bytes 4718600 | tf_op jit(solution)/shard_map/ppermute | solution.py:640
  1428.1 49.8 %collective-permute-start.30 = (f32[2,512,384]{2,1,0:T(8,128)}, f32[2,512,384]{2,1,0:T(8,128)}, u32[]{:S(2)}, u32[]{:S(2)}) collective-permute-start(f32[2,512,384]{2,1,0:T(8,128)} %get-tuple-element.130), channel_id=1, source_target_pairs={{0,2},{1,3},{2,0},{3,1},{4,6},{5,7},{6,4},{7,5},{8,10},{9,11},{10,... | collective-permute-start | bytes 4718600 | tf_op jit(solution)/shard_map/ppermute | solution.py:640
  1477.9 201.1 %all-reduce.11.cloned.1.call-done = f32[1164,128]{1,0:T(8,128)} async-done(((f32[1164,128]{1,0:T(8,128)}), f32[1164,128]{1,0:T(8,128)}) %all-reduce.11.cloned.1.call-update) | async-done | bytes 595984 | tf_op jit(solution)/shard_map/psum | solution.py:679
  1700.2 118.2 %collective-permute-done.34.refs_8_ = f32[2,512,384]{2,1,0:T(8,128)} collective-permute-done((f32[2,512,384]{2,1,0:T(8,128)}, f32[2,512,384]{2,1,0:T(8,128)}, u32[]{:S(2)}, u32[]{:S(2)}) %collective-permute-start.34) | collective-permute-done | bytes 1572896 | tf_op jit(solution)/shard_map/ppermute | solution.py:640
  1818.4 34.1 %collective-permute-done.38.refs_12_ = f32[2,512,384]{2,1,0:T(8,128)} collective-permute-done((f32[2,512,384]{2,1,0:T(8,128)}, f32[2,512,384]{2,1,0:T(8,128)}, u32[]{:S(2)}, u32[]{:S(2)}) %collective-permute-start.38) | collective-permute-done | bytes 1572896 | tf_op jit(solution)/shard_map/ppermute | solution.py:640
  (253 shorter events, 364.9 us)
Async XLA Ops:
  7.2 1671.9 %all-reduce.11.cloned.1.call-start = ((), (), s32[]{:S(2)}) async-start(), calls=%async_computation | async-start | bytes 1196032 | tf_op jit(solution)/shard_map/psum | solution.py:679
  32.5 189.6 %collective-permute-start.23 = (f32[2,512,384]{2,1,0:T(8,128)}, f32[2,512,384]{2,1,0:T(8,128)}, u32[]{:S(2)}, u32[]{:S(2)}) collective-permute-start(f32[2,512,384]{2,1,0:T(8,128)} %get-tuple-element.109), channel_id=1, source_target_pairs={{0,3},{1,0},{2,1},{3,2},{4,7},{5,4},{6,5},{7,6},{8,11},{9,8},{10,9... | collective-permute-start | bytes 4718600 | tf_op jit(solution)/shard_map/ppermute | solution.py:640
  33.9 218.9 %collective-permute-start.24 = (f32[2,512,384]{2,1,0:T(8,128)}, f32[2,512,384]{2,1,0:T(8,128)}, u32[]{:S(2)}, u32[]{:S(2)}) collective-permute-start(f32[2,512,384]{2,1,0:T(8,128)} %get-tuple-element.110), channel_id=1, source_target_pairs={{0,4},{1,5},{2,6},{3,7},{4,0},{5,1},{6,2},{7,3},{8,12},{9,13},{10,... | collective-permute-start | bytes 4718600 | tf_op jit(solution)/shard_map/ppermute | solution.py:640
  35.4 226.2 %collective-permute-start.25 = (f32[2,512,384]{2,1,0:T(8,128)}, f32[2,512,384]{2,1,0:T(8,128)}, u32[]{:S(2)}, u32[]{:S(2)}) collective-permute-start(f32[2,512,384]{2,1,0:T(8,128)} %get-tuple-element.111), channel_id=1, source_target_pairs={{0,5},{1,6},{2,7},{3,4},{4,1},{5,2},{6,3},{7,0},{8,13},{9,14},{10,... | collective-permute-start | bytes 4718600 | tf_op jit(solution)/shard_map/ppermute | solution.py:640
  75.7 261.7 %collective-permute-start.26 = (f32[2,512,384]{2,1,0:T(8,128)}, f32[2,512,384]{2,1,0:T(8,128)}, u32[]{:S(2)}, u32[]{:S(2)}) collective-permute-start(f32[2,512,384]{2,1,0:T(8,128)} %get-tuple-element.112), channel_id=1, source_target_pairs={{0,6},{1,7},{2,4},{3,5},{4,2},{5,3},{6,0},{7,1},{8,14},{9,15},{10,... | collective-permute-start | bytes 4718600 | tf_op jit(solution)/shard_map/ppermute | solution.py:640
  137.0 201.0 %collective-permute-start.27 = (f32[2,512,384]{2,1,0:T(8,128)}, f32[2,512,384]{2,1,0:T(8,128)}, u32[]{:S(2)}, u32[]{:S(2)}) collective-permute-start(f32[2,512,384]{2,1,0:T(8,128)} %get-tuple-element.113), channel_id=1, source_target_pairs={{0,7},{1,4},{2,5},{3,6},{4,3},{5,0},{6,1},{7,2},{8,15},{9,12},{10,... | collective-permute-start | bytes 4718600 | tf_op jit(solution)/shard_map/ppermute | solution.py:640
  252.8 218.6 %collective-permute-start.15 = (f32[2,512,384]{2,1,0:T(8,128)}, f32[2,512,384]{2,1,0:T(8,128)}, u32[]{:S(2)}, u32[]{:S(2)}) collective-permute-start(f32[2,512,384]{2,1,0:T(8,128)} %get-tuple-element.100), channel_id=1, source_target_pairs={{0,2},{1,3},{2,0},{3,1},{4,6},{5,7},{6,4},{7,5},{8,10},{9,11},{10,... | collective-permute-start | bytes 4718600 | tf_op jit(solution)/shard_map/ppermute | solution.py:640
  261.5 246.6 %collective-permute-start.16 = (f32[2,512,384]{2,1,0:T(8,128)}, f32[2,512,384]{2,1,0:T(8,128)S(1)}, u32[]{:S(2)}, u32[]{:S(2)}) collective-permute-start(f32[2,512,384]{2,1,0:T(8,128)} %get-tuple-element.101), channel_id=1, source_target_pairs={{0,3},{1,0},{2,1},{3,2},{4,7},{5,4},{6,5},{7,6},{8,11},{9,8},{10,9... | collective-permute-start | bytes 4718600 | tf_op jit(solution)/shard_map/ppermute | solution.py:640
  379.0 228.1 %collective-permute-start.19 = (f32[2,512,384]{2,1,0:T(8,128)}, f32[2,512,384]{2,1,0:T(8,128)}, u32[]{:S(2)}, u32[]{:S(2)}) collective-permute-start(f32[2,512,384]{2,1,0:T(8,128)} %get-tuple-element.104), channel_id=1, source_target_pairs={{0,6},{1,7},{2,4},{3,5},{4,2},{5,3},{6,0},{7,1},{8,14},{9,15},{10,... | collective-permute-start | bytes 4718600 | tf_op jit(solution)/shard_map/ppermute | solution.py:640
  508.1 204.4 %collective-permute-start.7 = (f32[2,512,384]{2,1,0:T(8,128)}, f32[2,512,384]{2,1,0:T(8,128)}, u32[]{:S(2)}, u32[]{:S(2)}) collective-permute-start(f32[2,512,384]{2,1,0:T(8,128)} %get-tuple-element.84), channel_id=1, source_target_pairs={{0,1},{1,2},{2,3},{3,0},{4,5},{5,6},{6,7},{7,4},{8,9},{9,10},{10,1... | collective-permute-start | bytes 4718600 | tf_op jit(solution)/shard_map/ppermute | solution.py:640
  508.2 208.7 %collective-permute-start.8 = (f32[2,512,384]{2,1,0:T(8,128)}, f32[2,512,384]{2,1,0:T(8,128)}, u32[]{:S(2)}, u32[]{:S(2)}) collective-permute-start(f32[2,512,384]{2,1,0:T(8,128)} %get-tuple-element.85), channel_id=1, source_target_pairs={{0,2},{1,3},{2,0},{3,1},{4,6},{5,7},{6,4},{7,5},{8,10},{9,11},{10,... | collective-permute-start | bytes 4718600 | tf_op jit(solution)/shard_map/ppermute | solution.py:640
  508.3 210.7 %collective-permute-start.9 = (f32[2,512,384]{2,1,0:T(8,128)}, f32[2,512,384]{2,1,0:T(8,128)}, u32[]{:S(2)}, u32[]{:S(2)}) collective-permute-start(f32[2,512,384]{2,1,0:T(8,128)} %get-tuple-element.86), channel_id=1, source_target_pairs={{0,3},{1,0},{2,1},{3,2},{4,7},{5,4},{6,5},{7,6},{8,11},{9,8},{10,9... | collective-permute-start | bytes 4718600 | tf_op jit(solution)/shard_map/ppermute | solution.py:640
  607.7 223.4 %collective-permute-start.11 = (f32[2,512,384]{2,1,0:T(8,128)}, f32[2,512,384]{2,1,0:T(8,128)}, u32[]{:S(2)}, u32[]{:S(2)}) collective-permute-start(f32[2,512,384]{2,1,0:T(8,128)} %get-tuple-element.88), channel_id=1, source_target_pairs={{0,5},{1,6},{2,7},{3,4},{4,1},{5,2},{6,3},{7,0},{8,13},{9,14},{10,... | collective-permute-start | bytes 4718600 | tf_op jit(solution)/shard_map/ppermute | solution.py:640
  719.1 224.8 %collective-permute-start = (f32[2,512,384]{2,1,0:T(8,128)}, f32[2,512,384]{2,1,0:T(8,128)}, u32[]{:S(2)}, u32[]{:S(2)}) collective-permute-start(f32[2,512,384]{2,1,0:T(8,128)} %get-tuple-element.76), channel_id=1, source_target_pairs={{0,1},{1,2},{2,3},{3,0},{4,5},{5,6},{6,7},{7,4},{8,9},{9,10},{10,1... | collective-permute-start | bytes 4718600 | tf_op jit(solution)/shard_map/ppermute | solution.py:640
  775.3 235.4 %collective-permute-start.1 = (f32[2,512,384]{2,1,0:T(8,128)}, f32[2,512,384]{2,1,0:T(8,128)}, u32[]{:S(2)}, u32[]{:S(2)}) collective-permute-start(f32[2,512,384]{2,1,0:T(8,128)} %get-tuple-element.77), channel_id=1, source_target_pairs={{0,2},{1,3},{2,0},{3,1},{4,6},{5,7},{6,4},{7,5},{8,10},{9,11},{10,... | collective-permute-start | bytes 4718600 | tf_op jit(solution)/shard_map/ppermute | solution.py:640
  831.1 230.8 %collective-permute-start.2 = (f32[2,512,384]{2,1,0:T(8,128)}, f32[2,512,384]{2,1,0:T(8,128)}, u32[]{:S(2)}, u32[]{:S(2)}) collective-permute-start(f32[2,512,384]{2,1,0:T(8,128)} %get-tuple-element.78), channel_id=1, source_target_pairs={{0,3},{1,0},{2,1},{3,2},{4,7},{5,4},{6,5},{7,6},{8,11},{9,8},{10,9... | collective-permute-start | bytes 4718600 | tf_op jit(solution)/shard_map/ppermute | solution.py:640
  876.9 185.1 %collective-permute-start.3 = (f32[2,512,384]{2,1,0:T(8,128)}, f32[2,512,384]{2,1,0:T(8,128)}, u32[]{:S(2)}, u32[]{:S(2)}) collective-permute-start(f32[2,512,384]{2,1,0:T(8,128)} %get-tuple-element.79), channel_id=1, source_target_pairs={{0,4},{1,5},{2,6},{3,7},{4,0},{5,1},{6,2},{7,3},{8,12},{9,13},{10,... | collective-permute-start | bytes 4718600 | tf_op jit(solution)/shard_map/ppermute | solution.py:640
  1239.0 189.2 %collective-permute-start.33 = (f32[2,512,384]{2,1,0:T(8,128)}, f32[2,512,384]{2,1,0:T(8,128)}, u32[]{:S(2)}, u32[]{:S(2)}) collective-permute-start(f32[2,512,384]{2,1,0:T(8,128)} %get-tuple-element.133), channel_id=1, source_target_pairs={{0,1},{1,2},{2,3},{3,0},{4,5},{5,6},{6,7},{7,4},{8,9},{9,10},{10,1... | collective-permute-start | bytes 4718600 | tf_op jit(solution)/shard_map/ppermute | solution.py:640
  1239.5 238.4 %collective-permute-start.35 = (f32[2,512,384]{2,1,0:T(8,128)}, f32[2,512,384]{2,1,0:T(8,128)}, u32[]{:S(2)}, u32[]{:S(2)}) collective-permute-start(f32[2,512,384]{2,1,0:T(8,128)} %get-tuple-element.135), channel_id=1, source_target_pairs={{0,4},{1,5},{2,6},{3,7},{4,0},{5,1},{6,2},{7,3},{8,12},{9,13},{10,... | collective-permute-start | bytes 4718600 | tf_op jit(solution)/shard_map/ppermute | solution.py:640
  1263.2 415.9 %collective-permute-start.37 = (f32[2,512,384]{2,1,0:T(8,128)}, f32[2,512,384]{2,1,0:T(8,128)}, u32[]{:S(2)}, u32[]{:S(2)}) collective-permute-start(f32[2,512,384]{2,1,0:T(8,128)} %get-tuple-element.137), channel_id=1, source_target_pairs={{0,7},{1,4},{2,5},{3,6},{4,3},{5,0},{6,1},{7,2},{8,15},{9,12},{10,... | collective-permute-start | bytes 4718600 | tf_op jit(solution)/shard_map/ppermute | solution.py:640
  1274.2 406.3 %collective-permute-start.39 = (f32[2,512,384]{2,1,0:T(8,128)}, f32[2,512,384]{2,1,0:T(8,128)}, u32[]{:S(2)}, u32[]{:S(2)}) collective-permute-start(f32[2,512,384]{2,1,0:T(8,128)} %get-tuple-element.139), channel_id=1, source_target_pairs={{0,6},{1,7},{2,4},{3,5},{4,2},{5,3},{6,0},{7,1},{8,14},{9,15},{10,... | collective-permute-start | bytes 4718600 | tf_op jit(solution)/shard_map/ppermute | solution.py:640
  1375.3 308.7 %collective-permute-start.28 = (f32[2,512,384]{2,1,0:T(8,128)}, f32[2,512,384]{2,1,0:T(8,128)}, u32[]{:S(2)}, u32[]{:S(2)}) collective-permute-start(f32[2,512,384]{2,1,0:T(8,128)} %get-tuple-element.128), channel_id=1, source_target_pairs={{0,3},{1,0},{2,1},{3,2},{4,7},{5,4},{6,5},{7,6},{8,11},{9,8},{10,9... | collective-permute-start | bytes 4718600 | tf_op jit(solution)/shard_map/ppermute | solution.py:640
  1428.1 257.4 %collective-permute-start.30 = (f32[2,512,384]{2,1,0:T(8,128)}, f32[2,512,384]{2,1,0:T(8,128)}, u32[]{:S(2)}, u32[]{:S(2)}) collective-permute-start(f32[2,512,384]{2,1,0:T(8,128)} %get-tuple-element.130), channel_id=1, source_target_pairs={{0,2},{1,3},{2,0},{3,1},{4,6},{5,7},{6,4},{7,5},{8,10},{9,11},{10,... | collective-permute-start | bytes 4718600 | tf_op jit(solution)/shard_map/ppermute | solution.py:640
  1477.9 208.2 %collective-permute-start.32 = (f32[2,512,384]{2,1,0:T(8,128)}, f32[2,512,384]{2,1,0:T(8,128)}, u32[]{:S(2)}, u32[]{:S(2)}) collective-permute-start(f32[2,512,384]{2,1,0:T(8,128)} %get-tuple-element.132), channel_id=1, source_target_pairs={{0,1},{1,2},{2,3},{3,0},{4,5},{5,6},{6,7},{7,4},{8,9},{9,10},{10,1... | collective-permute-start | bytes 4718600 | tf_op jit(solution)/shard_map/ppermute | solution.py:640
  (44 other events, 4560.7 us)
Sparse Core Ops, SparseCore 0:
  1478.0 200.9 all-reduce.10
